TPU v7x, 32 devices: a whole 2x2x4 slice. The times are simulated.
32 devices in a mesh: depth: 8 (over z, y), rows: 4 (over x, core).
Axes of the slice: x: 2, y: 2, z: 4, core: 2. Of those that a mesh axis runs over, the one named last changes fastest.
Arguments:
- density: float32 [16, 512, 512], P('depth', 'rows'), may hold values from 0 to 6
- transfer_table: float32 [4, 16], replicated, may hold values from 0.2 to 1
Outputs:
- picture: float32 [4, 512, 512], P(None, ('rows', 'depth'))
All inputs are finite; a program needn't handle non-finite values.
Results may differ from a plain program's by a relative error of at most 0.000021.
Values sent between devices are 32-bit elements; how exact they have to be, the bound alone decides.
A program may use at most 64 MiB of HBM per device.

v0:
```python
import jax
import jax.numpy as jnp
from jax import lax
from jax.sharding import PartitionSpec as P

PASSES = 3
KNOTS = 16


TIME_STEP = 0.15
OPTICAL_DEPTH = 3.0
UPPER_DENSITY = 6.0
AMBIENT = 0.35


def extended(cells, sides, width):
    for axis, dim in sides:
        count = lax.axis_size(axis)
        ends = count - 1
        head = lax.slice_in_dim(cells, 0, width, axis=dim)
        tail = lax.slice_in_dim(cells, cells.shape[dim] - width, cells.shape[dim], axis=dim)
        cells = jnp.concatenate(
            [
                lax.ppermute(tail, axis, [(i, (i + 1) % count) for i in range(ends)]),
                cells,
                lax.ppermute(head, axis, [((i + 1) % count, i) for i in range(ends)]),
            ],
            axis=dim,
        )
    return cells


def partner(value, axis, stride):
    mask = 2**stride
    pairs = [(source, source ^ mask) for source in range(lax.axis_size(axis))]
    return lax.ppermute(value, axis, pairs)


def diffusion_flux(center, neighbours):
    summed = jnp.zeros_like(center)
    for other in neighbours:
        change = other - center
        summed = summed + change / (1.0 + change * change)
    return center + TIME_STEP * summed


def appearance(center, neighbours, transfer_table, depth_count):
    deeper, nearer, next_row, prev_row, next_col, prev_col = neighbours
    grad_depth = (deeper - nearer) * 0.5
    grad_row = (next_row - prev_row) * 0.5
    grad_col = (next_col - prev_col) * 0.5
    shading = AMBIENT + (1.0 - AMBIENT) * jnp.abs(
        0.64 * grad_depth + 0.6 * grad_row + 0.48 * grad_col
    ) / jnp.sqrt(grad_depth * grad_depth + grad_row * grad_row + grad_col * grad_col + 0.25)
    position = center * ((KNOTS - 1) / UPPER_DENSITY)
    mixed = [jnp.zeros_like(center) for channel in range(4)]
    for knot in range(KNOTS):
        hat_weight = jnp.maximum(0.0, 1.0 - jnp.abs(position - knot))
        mixed = [
            mixed[channel] + transfer_table[channel, knot] * hat_weight for channel in range(4)
        ]
    opacity = 1.0 - jnp.exp(-mixed[3] * (OPTICAL_DEPTH / depth_count))
    colors = jnp.stack([mixed[0] * shading, mixed[1] * shading, mixed[2] * shading])
    return (colors, opacity)


def neighbour_fields(field):
    padded = extended(field, (("depth", 0), ("rows", 1)), 1)
    depth_index = lax.axis_index("depth")
    depth_count = lax.axis_size("depth")
    rows_index = lax.axis_index("rows")
    rows_count = lax.axis_size("rows")
    above = jnp.where(depth_index == 0, field[:1], padded[:1, 1:-1])
    below = jnp.where(depth_index == depth_count - 1, field[-1:], padded[-1:, 1:-1])
    first_row = jnp.where(rows_index == 0, field[:, :1], padded[1:-1, :1])
    last_row = jnp.where(rows_index == rows_count - 1, field[:, -1:], padded[1:-1, -1:])
    deeper = jnp.concatenate([field[1:], below], axis=0)
    nearer = jnp.concatenate([above, field[:-1]], axis=0)
    next_row = jnp.concatenate([field[:, 1:], last_row], axis=1)
    prev_row = jnp.concatenate([first_row, field[:, :-1]], axis=1)
    next_col = jnp.concatenate([field[:, :, 1:], field[:, :, -1:]], axis=2)
    prev_col = jnp.concatenate([field[:, :, :1], field[:, :, :-1]], axis=2)
    return (deeper, nearer, next_row, prev_row, next_col, prev_col)


def composite(front_part, back_part):
    return front_part + (1.0 - front_part[3:4]) * back_part


def per_device(density, transfer_table):
    planes_here = density.shape[0]
    band_rows = density.shape[1]
    columns = density.shape[2]
    depth_count = lax.axis_size("depth")
    depth_index = lax.axis_index("depth")
    total_planes = planes_here * depth_count
    field = density
    for sweep in range(PASSES):
        field = diffusion_flux(field, neighbour_fields(field))
    colors, opacity = appearance(field, neighbour_fields(field), transfer_table, total_planes)
    color_sum = jnp.zeros((3, band_rows, columns), jnp.float32)
    remaining = jnp.ones((band_rows, columns), jnp.float32)
    for plane in range(planes_here):
        color_sum = color_sum + remaining * opacity[plane] * colors[:, plane]
        remaining = remaining * (1.0 - opacity[plane])
    partial_value = jnp.concatenate([color_sum, (1.0 - remaining)[None]], axis=0)
    strip_rows = band_rows // depth_count
    current = partial_value.reshape(4, depth_count, strip_rows, columns)
    levels = depth_count.bit_length() - 1
    for bit in range(levels):
        blocks = current.shape[1]
        paired = current.reshape(4, blocks // 2, 2, strip_rows, columns)
        own_bit = depth_index // 2**bit % 2
        kept_half = jnp.where(own_bit == 0, paired[:, :, 0], paired[:, :, 1])
        sent_half = jnp.where(own_bit == 0, paired[:, :, 1], paired[:, :, 0])
        received = partner(sent_half, "depth", bit)
        front_part = jnp.where(own_bit == 0, kept_half, received)
        back_part = jnp.where(own_bit == 0, received, kept_half)
        current = composite(front_part, back_part)
    return current.reshape(4, strip_rows, columns)


def solution(mesh):
    placed = (P("depth", "rows", None), P())
    return jax.shard_map(
        per_device,
        mesh=mesh,
        in_specs=placed,
        out_specs=P(None, ("rows", "depth"), None),
        check_vma=False,
    )
```

profile of v0, /device:TPU:0, one launch (start us, length us, event | category | flops | bytes accessed | tf_op | source)
XLA Modules:
  0.0 178.6 jit_solution(12307767602227641219)
XLA Ops:
  1.2 1.4 collective-permute-start
  2.6 6.2 %collective-permute-start.1 = (f32[1,128,512]{2,1,0:T(8,128)S(1)}, f32[1,128,512]{2,1,0:T(8,128)}, u32[]{:S(2)}, u32[]{:S(2)}) collective-permute-start(f32[1,128,512]{2,1,0:T(8,128)S(1)} %get-tuple-element.65), channel_id=1, source_target_pairs={{0,4},{4,8},{8,12},{12,16},{16,20},{20,24},{24,28},{1,5},{5,9},{9,... | collective-permute-start | bytes 786440 | tf_op jit(solution)/shard_map/ppermute | solution.py:24
  12.5 5.8 %collective-permute-done.1 = f32[1,128,512]{2,1,0:T(8,128)} collective-permute-done((f32[1,128,512]{2,1,0:T(8,128)S(1)}, f32[1,128,512]{2,1,0:T(8,128)}, u32[]{:S(2)}, u32[]{:S(2)}) %collective-permute-start.1) | collective-permute-done | bytes 262176 | tf_op jit(solution)/shard_map/ppermute | solution.py:24
  19.4 1.3 collective-permute-start.2
  20.7 3.0 %collective-permute-start.3 = (f32[4,1,512]{2,1,0:T(1,128)S(1)}, f32[4,1,512]{2,1,0:T(1,128)S(1)}, u32[]{:S(2)}, u32[]{:S(2)}) collective-permute-start(f32[4,1,512]{2,1,0:T(1,128)S(1)} %get-tuple-element.18), channel_id=1, source_target_pairs={{0,1},{1,2},{2,3},{4,5},{5,6},{6,7},{8,9},{9,10},{10,11},{12,13},{... | collective-permute-start | bytes 24584 | tf_op jit(solution)/shard_map/ppermute | solution.py:24
  24.5 1.8 %multiply_add_fusion.5 = f32[2,128,512]{2,1,0:T(8,128)S(1)} fusion(f32[2,128,512]{2,1,0:T(8,128)S(1)} %copy-done, f32[2,128,511]{2,1,0:T(8,128)S(1)} %get-tuple-element.67, f32[2,128,1]{2,1,0:T(8,128)} %get-tuple-element.69, f32[2,128,1]{2,1,0:T(8,128)S(1)} %get-tuple-element.68, f32[2,128,511]{2,1,0:T(8,128)S(1)} %get-tuple-element.66, ...), kind=kLoop, calls=%fused_computation.54 | loop fusion | flops 4849664 | bytes 4194304 | tf_op jit(solution)/shard_map/add | solution.py:44
  26.6 1.3 collective-permute-start.4
  27.9 5.1 %collective-permute-start.5 = (f32[1,128,512]{2,1,0:T(8,128)S(1)}, f32[1,128,512]{2,1,0:T(8,128)S(1)}, u32[]{:S(2)}, u32[]{:S(2)}) collective-permute-start(f32[1,128,512]{2,1,0:T(8,128)S(1)} %get-tuple-element.52), channel_id=1, source_target_pairs={{0,4},{4,8},{8,12},{12,16},{16,20},{20,24},{24,28},{1,5},{5,9},{9,... | collective-permute-start | bytes 786440 | tf_op jit(solution)/shard_map/ppermute | solution.py:24
  33.3 4.5 %collective-permute-done.4 = f32[1,128,512]{2,1,0:T(8,128)S(1)} collective-permute-done((f32[1,128,512]{2,1,0:T(8,128)S(1)}, f32[1,128,512]{2,1,0:T(8,128)S(1)}, u32[]{:S(2)}, u32[]{:S(2)}) %collective-permute-start.4) | collective-permute-done | bytes 262176 | tf_op jit(solution)/shard_map/ppermute | solution.py:26
  37.8 6.5 %collective-permute-done.5 = f32[1,128,512]{2,1,0:T(8,128)S(1)} collective-permute-done((f32[1,128,512]{2,1,0:T(8,128)S(1)}, f32[1,128,512]{2,1,0:T(8,128)S(1)}, u32[]{:S(2)}, u32[]{:S(2)}) %collective-permute-start.5) | collective-permute-done | bytes 262176 | tf_op jit(solution)/shard_map/ppermute | solution.py:24
  44.3 1.3 collective-permute-start.6
  45.6 3.0 %collective-permute-start.7 = (f32[4,1,512]{2,1,0:T(1,128)S(1)}, f32[4,1,512]{2,1,0:T(1,128)S(1)}, u32[]{:S(2)}, u32[]{:S(2)}) collective-permute-start(f32[4,1,512]{2,1,0:T(1,128)S(1)} %get-tuple-element.16), channel_id=1, source_target_pairs={{0,1},{1,2},{2,3},{4,5},{5,6},{6,7},{8,9},{9,10},{10,11},{12,13},{... | collective-permute-start | bytes 24584 | tf_op jit(solution)/shard_map/ppermute | solution.py:24
  50.5 1.3 collective-permute-start.8
  51.8 5.0 %collective-permute-start.9 = (f32[1,128,512]{2,1,0:T(8,128)S(1)}, f32[1,128,512]{2,1,0:T(8,128)S(1)}, u32[]{:S(2)}, u32[]{:S(2)}) collective-permute-start(f32[1,128,512]{2,1,0:T(8,128)S(1)} %get-tuple-element.40), channel_id=1, source_target_pairs={{0,4},{4,8},{8,12},{12,16},{16,20},{20,24},{24,28},{1,5},{5,9},{9,... | collective-permute-start | bytes 786440 | tf_op jit(solution)/shard_map/ppermute | solution.py:24
  57.0 4.4 %collective-permute-done.8 = f32[1,128,512]{2,1,0:T(8,128)S(1)} collective-permute-done((f32[1,128,512]{2,1,0:T(8,128)S(1)}, f32[1,128,512]{2,1,0:T(8,128)S(1)}, u32[]{:S(2)}, u32[]{:S(2)}) %collective-permute-start.8) | collective-permute-done | bytes 262176 | tf_op jit(solution)/shard_map/ppermute | solution.py:26
  61.5 6.6 %collective-permute-done.9 = f32[1,128,512]{2,1,0:T(8,128)S(1)} collective-permute-done((f32[1,128,512]{2,1,0:T(8,128)S(1)}, f32[1,128,512]{2,1,0:T(8,128)S(1)}, u32[]{:S(2)}, u32[]{:S(2)}) %collective-permute-start.9) | collective-permute-done | bytes 262176 | tf_op jit(solution)/shard_map/ppermute | solution.py:24
  69.4 3.0 %collective-permute-start.11 = (f32[4,1,512]{2,1,0:T(1,128)S(1)}, f32[4,1,512]{2,1,0:T(1,128)S(1)}, u32[]{:S(2)}, u32[]{:S(2)}) collective-permute-start(f32[4,1,512]{2,1,0:T(1,128)S(1)} %get-tuple-element.14), channel_id=1, source_target_pairs={{0,1},{1,2},{2,3},{4,5},{5,6},{6,7},{8,9},{9,10},{10,11},{12,13},{... | collective-permute-start | bytes 24584 | tf_op jit(solution)/shard_map/ppermute | solution.py:24
  73.2 12.8 %exponential_subtract_fusion = (f32[2,128,512]{2,1,0:T(8,128)S(1)}, f32[2,128,512]{2,1,0:T(8,128)S(1)}) fusion(f32[]{:T(128)} %bitcast.15, f32[]{:T(128)} %bitcast.14, f32[]{:T(128)} %bitcast.13, f32[]{:T(128)} %bitcast.12, f32[]{:T(128)} %bitcast.11, f32[]{:T(128)} %bitcast.10, f32[]{:T(128)} %bitcast.9, f32[]{:T(128)} %bitcast.8, f32[]{:T(128)} %bitcast.7, ...), kind=kLoop, calls=%fused_computation.35 | loop fusion | flops 17694720 | bytes 4718656 | tf_op jit(solution)/shard_map/sub | solution.py:62
  86.3 1.3 collective-permute-start.12
  87.6 5.0 %collective-permute-start.13 = (f32[1,128,512]{2,1,0:T(8,128)S(1)}, f32[1,128,512]{2,1,0:T(8,128)S(1)}, u32[]{:S(2)}, u32[]{:S(2)}) collective-permute-start(f32[1,128,512]{2,1,0:T(8,128)S(1)} %get-tuple-element.28), channel_id=1, source_target_pairs={{0,4},{4,8},{8,12},{12,16},{16,20},{20,24},{24,28},{1,5},{5,9},{9,... | collective-permute-start | bytes 786440 | tf_op jit(solution)/shard_map/ppermute | solution.py:24
  92.9 4.4 %collective-permute-done.12 = f32[1,128,512]{2,1,0:T(8,128)S(1)} collective-permute-done((f32[1,128,512]{2,1,0:T(8,128)S(1)}, f32[1,128,512]{2,1,0:T(8,128)S(1)}, u32[]{:S(2)}, u32[]{:S(2)}) %collective-permute-start.12) | collective-permute-done | bytes 262176 | tf_op jit(solution)/shard_map/ppermute | solution.py:26
  97.3 6.6 %collective-permute-done.13 = f32[1,128,512]{2,1,0:T(8,128)S(1)} collective-permute-done((f32[1,128,512]{2,1,0:T(8,128)S(1)}, f32[1,128,512]{2,1,0:T(8,128)S(1)}, u32[]{:S(2)}, u32[]{:S(2)}) %collective-permute-start.13) | collective-permute-done | bytes 262176 | tf_op jit(solution)/shard_map/ppermute | solution.py:24
  105.2 3.2 %collective-permute-start.15 = (f32[4,1,512]{2,1,0:T(1,128)S(1)}, f32[4,1,512]{2,1,0:T(1,128)S(1)}, u32[]{:S(2)}, u32[]{:S(2)}) collective-permute-start(f32[4,1,512]{2,1,0:T(1,128)S(1)} %get-tuple-element.12), channel_id=1, source_target_pairs={{0,1},{1,2},{2,3},{4,5},{5,6},{6,7},{8,9},{9,10},{10,11},{12,13},{... | collective-permute-start | bytes 24584 | tf_op jit(solution)/shard_map/ppermute | solution.py:24
  109.1 12.1 %multiply_bitcast_fusion.2 = (f32[1,2,128,512]{3,2,0,1:T(8,128)S(1)}, f32[2,128,512]{2,1,0:T(8,128)S(1)}) fusion(f32[]{:T(128)} %bitcast.32, f32[]{:T(128)} %bitcast.31, f32[]{:T(128)} %bitcast.30, f32[]{:T(128)} %bitcast.29, f32[]{:T(128)} %bitcast.28, f32[]{:T(128)} %bitcast.27, f32[]{:T(128)} %bitcast.26, f32[]{:T(128)} %bitcast.25, f32[]{:T(128)} %bitcast.24, ...), kind=kLoop, calls=%fused_computation.33 | loop fusion | flops 16121856 | bytes 4718656 | tf_op jit(solution)/shard_map/stack | solution.py:63
  121.1 11.7 %multiply_bitcast_fusion.1 = f32[1,2,128,512]{3,2,0,1:T(8,128)S(1)} fusion(f32[2,128,512]{2,1,0:T(8,128)S(1)} %get-tuple-element.6, f32[]{:T(128)} %bitcast.50, f32[]{:T(128)} %bitcast.49, f32[]{:T(128)} %bitcast.48, f32[]{:T(128)} %bitcast.47, f32[]{:T(128)} %bitcast.46, f32[]{:T(128)} %bitcast.45, f32[]{:T(128)} %bitcast.44, f32[]{:T(128)} %bitcast.43, ...), kind=kLoop, calls=%fused_computation.32 | loop fusion | flops 12582912 | bytes 1572928 | tf_op jit(solution)/shard_map/stack | solution.py:63
  132.8 11.4 %multiply_bitcast_fusion = f32[1,2,128,512]{3,2,0,1:T(8,128)S(1)} fusion(f32[2,128,512]{2,1,0:T(8,128)S(1)} %get-tuple-element.6, f32[]{:T(128)} %bitcast.68, f32[]{:T(128)} %bitcast.67, f32[]{:T(128)} %bitcast.66, f32[]{:T(128)} %bitcast.65, f32[]{:T(128)} %bitcast.64, f32[]{:T(128)} %bitcast.63, f32[]{:T(128)} %bitcast.62, f32[]{:T(128)} %bitcast.61, ...), kind=kLoop, calls=%fused_computation.31 | loop fusion | flops 12582912 | bytes 1572928 | tf_op jit(solution)/shard_map/stack | solution.py:63
  145.0 2.5 %collective-permute-start.16 = (f32[4,4,16,512]{3,2,1,0:T(8,128)S(1)}, f32[4,4,16,512]{3,2,1,0:T(8,128)S(1)}, u32[]{:S(2)}, u32[]{:S(2)}) collective-permute-start(f32[4,4,16,512]{3,2,1,0:T(8,128)S(1)} %select_bitcast_fusion), channel_id=1, source_target_pairs={{0,4},{4,0},{8,12},{12,8},{16,20},{20,16},{24,28},{28,24},{1,5},{5... | collective-permute-start | bytes 1572872 | tf_op jit(solution)/shard_map/ppermute | solution.py:36
  147.5 12.2 %collective-permute-done.16 = f32[4,4,16,512]{3,2,1,0:T(8,128)S(1)} collective-permute-done((f32[4,4,16,512]{3,2,1,0:T(8,128)S(1)}, f32[4,4,16,512]{3,2,1,0:T(8,128)S(1)}, u32[]{:S(2)}, u32[]{:S(2)}) %collective-permute-start.16) | collective-permute-done | bytes 524320 | tf_op jit(solution)/shard_map/ppermute | solution.py:36
  160.1 1.6 collective-permute-start.17
  161.8 7.1 %collective-permute-done.17 = f32[4,2,16,512]{3,2,1,0:T(8,128)S(1)} collective-permute-done((f32[4,2,16,512]{3,2,1,0:T(8,128)S(1)}, f32[4,2,16,512]{3,2,1,0:T(8,128)S(1)}, u32[]{:S(2)}, u32[]{:S(2)}) %collective-permute-start.17) | collective-permute-done | bytes 262176 | tf_op jit(solution)/shard_map/ppermute | solution.py:36
  169.0 2.7 %collective-permute-start.18 = (f32[4,1,16,512]{3,2,0,1:T(8,128)S(1)}, f32[4,1,16,512]{3,2,0,1:T(8,128)S(1)}, u32[]{:S(2)}, u32[]{:S(2)}) collective-permute-start(f32[4,1,16,512]{3,2,0,1:T(8,128)S(1)} %select_bitcast_fusion.2), channel_id=1, source_target_pairs={{0,16},{4,20},{8,24},{12,28},{16,0},{20,4},{24,8},{28,12},{1,17},{... | collective-permute-start | bytes 393224 | tf_op jit(solution)/shard_map/ppermute | solution.py:36
  171.7 6.2 %collective-permute-done.18 = f32[4,1,16,512]{3,2,0,1:T(8,128)S(1)} collective-permute-done((f32[4,1,16,512]{3,2,0,1:T(8,128)S(1)}, f32[4,1,16,512]{3,2,0,1:T(8,128)S(1)}, u32[]{:S(2)}, u32[]{:S(2)}) %collective-permute-start.18) | collective-permute-done | bytes 131104 | tf_op jit(solution)/shard_map/ppermute | solution.py:36
  (70 shorter events, 15.6 us)
Async XLA Ops:
  0.0 8.8 %copy-start = (f32[2,128,512]{2,1,0:T(8,128)S(1)}, f32[2,128,512]{2,1,0:T(8,128)}, u32[]{:S(2)}) copy-start(f32[2,128,512]{2,1,0:T(8,128)} %param.2) | copy-start | bytes 1572868
  1.1 10.9 %copy-start.1 = (f32[1,128,512]{2,1,0:T(8,128)}, f32[1,128,512]{2,1,0:T(8,128)S(1)}, u32[]{:S(2)}) copy-start(f32[1,128,512]{2,1,0:T(8,128)S(1)} %get-tuple-element.64) | copy-start | bytes 786436
  1.1 10.9 %copy-start.2 = (f32[1,128,512]{2,1,0:T(8,128)}, f32[1,128,512]{2,1,0:T(8,128)S(1)}, u32[]{:S(2)}) copy-start(f32[1,128,512]{2,1,0:T(8,128)S(1)} %get-tuple-element.65) | copy-start | bytes 786436
  1.1 8.5 %copy-start.3 = (f32[4,16]{1,0:T(4,128)S(1)}, f32[4,16]{1,0:T(4,128)}, u32[]{:S(2)}) copy-start(f32[4,16]{1,0:T(4,128)} %param.3) | copy-start | bytes 772
  1.2 11.3 %collective-permute-start = (f32[1,128,512]{2,1,0:T(8,128)S(1)}, f32[1,128,512]{2,1,0:T(8,128)S(1)}, u32[]{:S(2)}, u32[]{:S(2)}) collective-permute-start(f32[1,128,512]{2,1,0:T(8,128)S(1)} %get-tuple-element.64), channel_id=1, source_target_pairs={{4,0},{8,4},{12,8},{16,12},{20,16},{24,20},{28,24},{5,1},{9,5},{13... | collective-permute-start | bytes 786440 | tf_op jit(solution)/shard_map/ppermute | solution.py:26
  2.6 15.6 %collective-permute-start.1 = (f32[1,128,512]{2,1,0:T(8,128)S(1)}, f32[1,128,512]{2,1,0:T(8,128)}, u32[]{:S(2)}, u32[]{:S(2)}) collective-permute-start(f32[1,128,512]{2,1,0:T(8,128)S(1)} %get-tuple-element.65), channel_id=1, source_target_pairs={{0,4},{4,8},{8,12},{12,16},{16,20},{20,24},{24,28},{1,5},{5,9},{9,... | collective-permute-start | bytes 786440 | tf_op jit(solution)/shard_map/ppermute | solution.py:24
  19.4 5.0 %collective-permute-start.2 = (f32[4,1,512]{2,1,0:T(1,128)S(1)}, f32[4,1,512]{2,1,0:T(1,128)S(1)}, u32[]{:S(2)}, u32[]{:S(2)}) collective-permute-start(f32[4,1,512]{2,1,0:T(1,128)S(1)} %get-tuple-element.17), channel_id=1, source_target_pairs={{1,0},{2,1},{3,2},{5,4},{6,5},{7,6},{9,8},{10,9},{11,10},{13,12},{... | collective-permute-start | bytes 24584 | tf_op jit(solution)/shard_map/ppermute | solution.py:26
  20.7 3.8 %collective-permute-start.3 = (f32[4,1,512]{2,1,0:T(1,128)S(1)}, f32[4,1,512]{2,1,0:T(1,128)S(1)}, u32[]{:S(2)}, u32[]{:S(2)}) collective-permute-start(f32[4,1,512]{2,1,0:T(1,128)S(1)} %get-tuple-element.18), channel_id=1, source_target_pairs={{0,1},{1,2},{2,3},{4,5},{5,6},{6,7},{8,9},{9,10},{10,11},{12,13},{... | collective-permute-start | bytes 24584 | tf_op jit(solution)/shard_map/ppermute | solution.py:24
  26.6 11.2 %collective-permute-start.4 = (f32[1,128,512]{2,1,0:T(8,128)S(1)}, f32[1,128,512]{2,1,0:T(8,128)S(1)}, u32[]{:S(2)}, u32[]{:S(2)}) collective-permute-start(f32[1,128,512]{2,1,0:T(8,128)S(1)} %get-tuple-element.53), channel_id=1, source_target_pairs={{4,0},{8,4},{12,8},{16,12},{20,16},{24,20},{28,24},{5,1},{9,5},{13... | collective-permute-start | bytes 786440 | tf_op jit(solution)/shard_map/ppermute | solution.py:26
  27.9 16.4 %collective-permute-start.5 = (f32[1,128,512]{2,1,0:T(8,128)S(1)}, f32[1,128,512]{2,1,0:T(8,128)S(1)}, u32[]{:S(2)}, u32[]{:S(2)}) collective-permute-start(f32[1,128,512]{2,1,0:T(8,128)S(1)} %get-tuple-element.52), channel_id=1, source_target_pairs={{0,4},{4,8},{8,12},{12,16},{16,20},{20,24},{24,28},{1,5},{5,9},{9,... | collective-permute-start | bytes 786440 | tf_op jit(solution)/shard_map/ppermute | solution.py:24
  44.3 4.4 %collective-permute-start.6 = (f32[4,1,512]{2,1,0:T(1,128)S(1)}, f32[4,1,512]{2,1,0:T(1,128)S(1)}, u32[]{:S(2)}, u32[]{:S(2)}) collective-permute-start(f32[4,1,512]{2,1,0:T(1,128)S(1)} %get-tuple-element.15), channel_id=1, source_target_pairs={{1,0},{2,1},{3,2},{5,4},{6,5},{7,6},{9,8},{10,9},{11,10},{13,12},{... | collective-permute-start | bytes 24584 | tf_op jit(solution)/shard_map/ppermute | solution.py:26
  45.6 3.8 %collective-permute-start.7 = (f32[4,1,512]{2,1,0:T(1,128)S(1)}, f32[4,1,512]{2,1,0:T(1,128)S(1)}, u32[]{:S(2)}, u32[]{:S(2)}) collective-permute-start(f32[4,1,512]{2,1,0:T(1,128)S(1)} %get-tuple-element.16), channel_id=1, source_target_pairs={{0,1},{1,2},{2,3},{4,5},{5,6},{6,7},{8,9},{9,10},{10,11},{12,13},{... | collective-permute-start | bytes 24584 | tf_op jit(solution)/shard_map/ppermute | solution.py:24
  50.5 11.0 %collective-permute-start.8 = (f32[1,128,512]{2,1,0:T(8,128)S(1)}, f32[1,128,512]{2,1,0:T(8,128)S(1)}, u32[]{:S(2)}, u32[]{:S(2)}) collective-permute-start(f32[1,128,512]{2,1,0:T(8,128)S(1)} %get-tuple-element.41), channel_id=1, source_target_pairs={{4,0},{8,4},{12,8},{16,12},{20,16},{24,20},{28,24},{5,1},{9,5},{13... | collective-permute-start | bytes 786440 | tf_op jit(solution)/shard_map/ppermute | solution.py:26
  51.8 16.3 %collective-permute-start.9 = (f32[1,128,512]{2,1,0:T(8,128)S(1)}, f32[1,128,512]{2,1,0:T(8,128)S(1)}, u32[]{:S(2)}, u32[]{:S(2)}) collective-permute-start(f32[1,128,512]{2,1,0:T(8,128)S(1)} %get-tuple-element.40), channel_id=1, source_target_pairs={{0,4},{4,8},{8,12},{12,16},{16,20},{20,24},{24,28},{1,5},{5,9},{9,... | collective-permute-start | bytes 786440 | tf_op jit(solution)/shard_map/ppermute | solution.py:24
  68.1 4.4 %collective-permute-start.10 = (f32[4,1,512]{2,1,0:T(1,128)S(1)}, f32[4,1,512]{2,1,0:T(1,128)S(1)}, u32[]{:S(2)}, u32[]{:S(2)}) collective-permute-start(f32[4,1,512]{2,1,0:T(1,128)S(1)} %get-tuple-element.13), channel_id=1, source_target_pairs={{1,0},{2,1},{3,2},{5,4},{6,5},{7,6},{9,8},{10,9},{11,10},{13,12},{... | collective-permute-start | bytes 24584 | tf_op jit(solution)/shard_map/ppermute | solution.py:26
  69.4 3.8 %collective-permute-start.11 = (f32[4,1,512]{2,1,0:T(1,128)S(1)}, f32[4,1,512]{2,1,0:T(1,128)S(1)}, u32[]{:S(2)}, u32[]{:S(2)}) collective-permute-start(f32[4,1,512]{2,1,0:T(1,128)S(1)} %get-tuple-element.14), channel_id=1, source_target_pairs={{0,1},{1,2},{2,3},{4,5},{5,6},{6,7},{8,9},{9,10},{10,11},{12,13},{... | collective-permute-start | bytes 24584 | tf_op jit(solution)/shard_map/ppermute | solution.py:24
  86.3 11.0 %collective-permute-start.12 = (f32[1,128,512]{2,1,0:T(8,128)S(1)}, f32[1,128,512]{2,1,0:T(8,128)S(1)}, u32[]{:S(2)}, u32[]{:S(2)}) collective-permute-start(f32[1,128,512]{2,1,0:T(8,128)S(1)} %get-tuple-element.29), channel_id=1, source_target_pairs={{4,0},{8,4},{12,8},{16,12},{20,16},{24,20},{28,24},{5,1},{9,5},{13... | collective-permute-start | bytes 786440 | tf_op jit(solution)/shard_map/ppermute | solution.py:26
  87.6 16.3 %collective-permute-start.13 = (f32[1,128,512]{2,1,0:T(8,128)S(1)}, f32[1,128,512]{2,1,0:T(8,128)S(1)}, u32[]{:S(2)}, u32[]{:S(2)}) collective-permute-start(f32[1,128,512]{2,1,0:T(8,128)S(1)} %get-tuple-element.28), channel_id=1, source_target_pairs={{0,4},{4,8},{8,12},{12,16},{16,20},{20,24},{24,28},{1,5},{5,9},{9,... | collective-permute-start | bytes 786440 | tf_op jit(solution)/shard_map/ppermute | solution.py:24
  103.9 4.6 %collective-permute-start.14 = (f32[4,1,512]{2,1,0:T(1,128)S(1)}, f32[4,1,512]{2,1,0:T(1,128)S(1)}, u32[]{:S(2)}, u32[]{:S(2)}) collective-permute-start(f32[4,1,512]{2,1,0:T(1,128)S(1)} %get-tuple-element.11), channel_id=1, source_target_pairs={{1,0},{2,1},{3,2},{5,4},{6,5},{7,6},{9,8},{10,9},{11,10},{13,12},{... | collective-permute-start | bytes 24584 | tf_op jit(solution)/shard_map/ppermute | solution.py:26
  105.2 3.8 %collective-permute-start.15 = (f32[4,1,512]{2,1,0:T(1,128)S(1)}, f32[4,1,512]{2,1,0:T(1,128)S(1)}, u32[]{:S(2)}, u32[]{:S(2)}) collective-permute-start(f32[4,1,512]{2,1,0:T(1,128)S(1)} %get-tuple-element.12), channel_id=1, source_target_pairs={{0,1},{1,2},{2,3},{4,5},{5,6},{6,7},{8,9},{9,10},{10,11},{12,13},{... | collective-permute-start | bytes 24584 | tf_op jit(solution)/shard_map/ppermute | solution.py:24
  145.0 14.7 %collective-permute-start.16 = (f32[4,4,16,512]{3,2,1,0:T(8,128)S(1)}, f32[4,4,16,512]{3,2,1,0:T(8,128)S(1)}, u32[]{:S(2)}, u32[]{:S(2)}) collective-permute-start(f32[4,4,16,512]{3,2,1,0:T(8,128)S(1)} %select_bitcast_fusion), channel_id=1, source_target_pairs={{0,4},{4,0},{8,12},{12,8},{16,20},{20,16},{24,28},{28,24},{1,5},{5... | collective-permute-start | bytes 1572872 | tf_op jit(solution)/shard_map/ppermute | solution.py:36
  160.1 8.7 %collective-permute-start.17 = (f32[4,2,16,512]{3,2,1,0:T(8,128)S(1)}, f32[4,2,16,512]{3,2,1,0:T(8,128)S(1)}, u32[]{:S(2)}, u32[]{:S(2)}) collective-permute-start(f32[4,2,16,512]{3,2,1,0:T(8,128)S(1)} %select_bitcast_fusion.1), channel_id=1, source_target_pairs={{0,8},{4,12},{8,0},{12,4},{16,24},{20,28},{24,16},{28,20},{1,9},{5... | collective-permute-start | bytes 786440 | tf_op jit(solution)/shard_map/ppermute | solution.py:36
  169.0 8.8 %collective-permute-start.18 = (f32[4,1,16,512]{3,2,0,1:T(8,128)S(1)}, f32[4,1,16,512]{3,2,0,1:T(8,128)S(1)}, u32[]{:S(2)}, u32[]{:S(2)}) collective-permute-start(f32[4,1,16,512]{3,2,0,1:T(8,128)S(1)} %select_bitcast_fusion.2), channel_id=1, source_target_pairs={{0,16},{4,20},{8,24},{12,28},{16,0},{20,4},{24,8},{28,12},{1,17},{... | collective-permute-start | bytes 393224 | tf_op jit(solution)/shard_map/ppermute | solution.py:36
where the time goes:
time: 180 us; the launch traced here: 179 us
  waiting for transfers between devices  66.7 us (37%)
  other arithmetic  53.8 us (30%)
  starting transfers between devices  51 us (28%)
  local copies, waits for them, and re-layouts  6.58 us (4%)
    another operation x4, other arithmetic, appearance(): jnp.stack([mixed[0] * shading, mixed[1] * shading, mixed[2] * shading])  35.3 us
    ppermute x8, starting transfers between devices, extended(): lax.ppermute(tail, axis, [(i, (i + 1) % count) for i in range(ends)])  33.7 us
    ppermute x8, waiting for transfers between devices, extended(): lax.ppermute(tail, axis, [(i, (i + 1) % count) for i in range(ends)])  27.5 us
    ppermute x3, waiting for transfers between devices, partner(): return lax.ppermute(value, axis, pairs)  25.4 us
    ppermute x8, waiting for transfers between devices, extended(): lax.ppermute(head, axis, [((i + 1) % count, i) for i in range(ends)])  13.7 us
    sub x1, other arithmetic, appearance(): opacity = 1.0 - jnp.exp(-mixed[3] * (OPTICAL_DEPTH / depth_count))  12.8 us
    ppermute x8, starting transfers between devices, extended(): lax.ppermute(head, axis, [((i + 1) % count, i) for i in range(ends)])  10.5 us
    ppermute x3, starting transfers between devices, partner(): return lax.ppermute(value, axis, pairs)  6.84 us
  transfers between devices with their start and end apart: 19, of which 15 were waited for; matrix products, arithmetic and copies ran while one was open for 3% of the time, Pallas kernels for 0%

commit v1 on v0

--- a/solution.py
+++ b/solution.py
@@ -1,6 +1,10 @@
+import functools
+
 import jax
 import jax.numpy as jnp
 from jax import lax
+from jax.experimental import pallas as pl
+from jax.experimental.pallas import tpu as pltpu
 from jax.sharding import PartitionSpec as P
 
 PASSES = 3
@@ -120,10 +124,378 @@
     return current.reshape(4, strip_rows, columns)
 
 
+HALO = PASSES + 1
+TILE = 8
+LANES = 128
+UNROLL = 4
+
+
+def flux(change):
+    denominator = 1.0 + change * change
+    guess = pl.reciprocal(denominator, approx=True)
+    return change * (guess * (2.0 - denominator * guess))
+
+
+def roll(cells, shift, axis):
+    return pltpu.roll(cells, shift % cells.shape[axis], axis)
+
+
+def lookup(entries, index):
+    return jnp.take_along_axis(entries, index, axis=1)
+
+
+def volume_kernel(
+    depth_count,
+    rows_count,
+    density,
+    transfer_table,
+    picture,
+    local,
+    table,
+    parcels,
+    edges,
+    field,
+    later,
+    rolled,
+    side,
+    knots,
+    shifted,
+    load_sem,
+    table_sem,
+    send,
+    recv,
+    edge_send,
+    edge_recv,
+):
+    planes, band, columns = local.shape
+    strip = band // depth_count
+    chunks = columns // LANES
+    total_planes = planes * depth_count
+    tall = strip + TILE
+    d = lax.axis_index("depth")
+    r = lax.axis_index("rows")
+    next_rows = lax.rem(r + 1, rows_count)
+    prev_rows = lax.rem(r + rows_count - 1, rows_count)
+    order = sorted(range(1, depth_count), key=lambda k: abs(k - depth_count // 2))
+
+    load = pltpu.make_async_copy(density, local, load_sem)
+    load.start()
+    load_table = pltpu.make_async_copy(transfer_table, table, table_sem)
+    load_table.start()
+
+    barrier = pltpu.get_barrier_semaphore()
+
+    def greet(depth, rows):
+        pl.semaphore_signal(
+            barrier, inc=1, device_id=(depth, rows), device_id_type=pl.DeviceIdType.MESH
+        )
+
+    for k in order:
+        greet(lax.rem(d + k, depth_count), r)
+
+    @pl.when(d == 0)
+    def _():
+        for s in range(depth_count):
+            greet(s, prev_rows)
+
+    @pl.when(d == depth_count - 1)
+    def _():
+        for s in range(depth_count):
+            greet(s, next_rows)
+
+    def flipped(rows, first):
+        return jnp.concatenate([rows[first - i : first - i + 1] for i in range(HALO)], axis=0)
+
+    load.wait()
+    for c in range(chunks):
+        lanes = slice(c * LANES, (c + 1) * LANES)
+        for p in range(planes):
+            first = local[p, :TILE, lanes]
+            final = local[p, band - TILE :, lanes]
+            edges[depth_count, p, c] = jnp.concatenate([first[:HALO], final[HALO:]], axis=0)
+            for s in range(depth_count):
+                parcels[s, c, p, :strip, :] = local[p, s * strip : (s + 1) * strip, lanes]
+                if s == 0:
+                    before = flipped(first, HALO - 1)
+                else:
+                    before = local[p, s * strip - TILE : s * strip, lanes][HALO:]
+                if s == depth_count - 1:
+                    after = flipped(final, TILE - 1)
+                else:
+                    after = local[p, (s + 1) * strip : (s + 1) * strip + TILE, lanes][:HALO]
+                parcels[s, c, p, strip:, :] = jnp.concatenate([after, before], axis=0)
+
+    def parcel(peer, c, slot):
+        return pltpu.make_async_remote_copy(
+            src_ref=parcels.at[peer, c],
+            dst_ref=field.at[c, pl.ds(d * planes, planes)],
+            send_sem=send.at[slot, c],
+            recv_sem=recv.at[d, c],
+            device_id=(peer, r),
+            device_id_type=pl.DeviceIdType.MESH,
+        )
+
+    def edge_copies():
+        return [
+            pltpu.make_async_remote_copy(
+                src_ref=edges.at[depth_count],
+                dst_ref=edges.at[d],
+                send_sem=edge_send.at[slot],
+                recv_sem=edge_recv.at[d],
+                device_id=(depth, rows),
+                device_id_type=pl.DeviceIdType.MESH,
+            )
+            for slot, depth, rows in ((0, depth_count - 1, prev_rows), (1, 0, next_rows))
+        ]
+
+    def landing(ref, sem):
+        return pltpu.make_async_copy(ref, ref, sem)
+
+    pl.semaphore_wait(barrier, depth_count + 1)
+    for copy in edge_copies():
+        copy.start()
+    for c in range(chunks):
+        for k in order:
+            parcel(lax.rem(d + k, depth_count), c, k).start()
+
+    for c in range(chunks):
+        for p in range(planes):
+            field[c, d * planes + p] = parcels[d, c, p]
+    dark = jnp.zeros((tall, LANES), jnp.float32)
+
+    @pl.loop(0, total_planes + 1)
+    def _(z):
+        field[chunks, z] = dark
+        for p in range(PASSES + 1):
+            rolled[p, z] = dark
+            side[p, z] = dark
+
+    load_table.wait()
+    entry = lax.broadcasted_iota(jnp.int32, (TILE, LANES), 1)
+    for channel in range(4):
+        value = jnp.zeros((TILE, LANES), jnp.float32)
+        slope = jnp.zeros((TILE, LANES), jnp.float32)
+        for knot in range(KNOTS - 1):
+            start = table[channel, knot]
+            value = jnp.where(entry == knot, start, value)
+            slope = jnp.where(entry == knot, table[channel, knot + 1] - start, slope)
+        knots[channel] = value
+        knots[4 + channel] = slope
+
+    lane = lax.broadcasted_iota(jnp.int32, (tall, LANES), 1)
+    lane_zero = lane == 0
+    upper = lax.broadcasted_iota(jnp.int32, (TILE, LANES), 0) < HALO
+
+    def merge(c, replaced):
+        for s in range(depth_count):
+            for p in range(planes):
+                z = s * planes + p
+                field[c, z, strip:, :] = jnp.where(
+                    replaced, edges[s, p, c], field[c, z, strip:, :]
+                )
+
+    @pl.when((d == 0) | (d == depth_count - 1))
+    def _():
+        for s in range(depth_count):
+            landing(edges.at[s], edge_recv.at[s]).wait()
+
+    def stage(c, p):
+        low = jnp.where(c == 0, p, -1)
+        high = jnp.where(c == chunks, p, LANES)
+        inner = (lane > low) & (lane < high)
+
+        def cells(z):
+            here = field[c, z] if p == 0 else later[p - 1, z]
+            moved = roll(here, 1, 1)
+            center = jnp.where(lane_zero, rolled[p, z], moved)
+            rolled[p, z] = moved
+            return here, center
+
+        def sides(z, value):
+            value = jnp.where(inner, value, 0.0)
+            moved = roll(value, 1, 1)
+            before = jnp.where(lane_zero, side[p, z], moved)
+            side[p, z] = moved
+            return value, before
+
+        return cells, sides
+
+    def diffuse(c, p):
+        cells, sides = stage(c, p)
+
+        def plane(z, carry):
+            here, center, above = carry
+            here_below, center_below = cells(z + 1)
+            below = flux(center_below - center)
+            down = flux(roll(center, -1, 0) - center)
+            right, left = sides(z, flux(here - center))
+            summed = (below - above) + (down - roll(down, 1, 0)) + (right - left)
+            result = center + TIME_STEP * summed
+            later[p, z] = result
+            return (here_below, center_below, below), result
+
+        def step(block, carry):
+            for u in range(UNROLL):
+                carry, result = plane(block * UNROLL + u, carry)
+
+            @pl.when(block == total_planes // UNROLL - 1)
+            def _():
+                later[p, total_planes] = result
+
+            return carry
+
+        here, center = cells(0)
+        lax.fori_loop(0, total_planes // UNROLL, step, (here, center, dark))
+
+    def shade(c):
+        cells, sides = stage(c, PASSES)
+
+        def plane(z, carry):
+            here, center, nearer, remaining, colors = carry
+            here_below, center_below = cells(z + 1)
+            down = roll(center, -1, 0) - center
+            right, left = sides(z, here - center)
+            middle = center[:strip]
+            grad_depth = (center_below[:strip] - nearer) * 0.5
+            grad_row = (down + roll(down, 1, 0))[:strip] * 0.5
+            grad_col = (right + left)[:strip] * 0.5
+            shading = AMBIENT + (1.0 - AMBIENT) * jnp.abs(
+                0.64 * grad_depth + 0.6 * grad_row + 0.48 * grad_col
+            ) * lax.rsqrt(
+                grad_depth * grad_depth + grad_row * grad_row + grad_col * grad_col + 0.25
+            )
+            position = middle * ((KNOTS - 1) / UPPER_DENSITY)
+            index = jnp.clip(position.astype(jnp.int32), 0, KNOTS - 2)
+            part = position - index.astype(jnp.float32)
+            tiles = [index[i : i + TILE] for i in range(0, strip, TILE)]
+            mixed = [
+                jnp.concatenate([lookup(knots[channel], tile) for tile in tiles], axis=0)
+                + part
+                * jnp.concatenate([lookup(knots[4 + channel], tile) for tile in tiles], axis=0)
+                for channel in range(4)
+            ]
+            through = jnp.exp(mixed[3] * (-OPTICAL_DEPTH / total_planes))
+            kept = remaining * through
+            weight = (remaining - kept) * shading
+            colors = tuple(colors[i] + weight * mixed[i] for i in range(3))
+            return here_below, center_below, middle, kept, colors
+
+        def step(block, carry):
+            for u in range(UNROLL):
+                carry = plane(block * UNROLL + u, carry)
+            return carry
+
+        here, center = cells(0)
+        flat = jnp.zeros((strip, LANES), jnp.float32)
+        carry = (here, center, center[:strip], jnp.ones_like(flat), (flat,) * 3)
+        carry = lax.fori_loop(0, total_planes // UNROLL, step, carry)
+        for channel in range(3):
+            shifted[c, channel] = carry[4][channel]
+        shifted[c, 3] = 1.0 - carry[3]
+
+    @pl.loop(0, chunks + 1)
+    def _(c):
+        @pl.when(c < chunks)
+        def _():
+            for k in order:
+                source = lax.rem(d + k, depth_count)
+                landing(
+                    field.at[c, pl.ds(source * planes, planes)], recv.at[source, c]
+                ).wait()
+
+            @pl.when(d == 0)
+            def _():
+                merge(c, jnp.logical_and(jnp.logical_not(upper), r > 0))
+
+            @pl.when(d == depth_count - 1)
+            def _():
+                merge(c, jnp.logical_and(upper, r < rows_count - 1))
+
+            field[c, total_planes] = field[c, total_planes - 1]
+
+        for p in range(PASSES):
+            diffuse(c, p)
+        shade(c)
+
+    early = lax.broadcasted_iota(jnp.int32, (strip, LANES), 1) < LANES - HALO
+    for c in range(chunks):
+        for channel in range(4):
+            picture[channel, :, c * LANES : (c + 1) * LANES] = jnp.where(
+                early,
+                roll(shifted[c, channel], -HALO, 1),
+                roll(shifted[c + 1, channel], -HALO, 1),
+            )
+
+    for c in range(chunks):
+        for k in order:
+            parcel(lax.rem(d + k, depth_count), c, k).wait_send()
+    for copy in edge_copies():
+        copy.wait_send()
+
+
+def in_one_kernel(depth_count, rows_count, density, transfer_table):
+    planes, band, columns = density.shape
+    strip = band // depth_count
+    chunks = columns // LANES
+    total_planes = planes * depth_count
+    tall = strip + TILE
+    return pl.pallas_call(
+        functools.partial(volume_kernel, depth_count, rows_count),
+        out_shape=jax.ShapeDtypeStruct((4, strip, columns), jnp.float32),
+        in_specs=[pl.BlockSpec(memory_space=pl.ANY)] * 2,
+        out_specs=pl.BlockSpec(memory_space=pltpu.VMEM),
+        scratch_shapes=[
+            pltpu.VMEM((planes, band, columns), jnp.float32),
+            pltpu.SMEM(transfer_table.shape, jnp.float32),
+            pltpu.VMEM((depth_count, chunks, planes, tall, LANES), jnp.float32),
+            pltpu.VMEM((depth_count + 1, planes, chunks, TILE, LANES), jnp.float32),
+            pltpu.VMEM((chunks + 1, total_planes + 1, tall, LANES), jnp.float32),
+            pltpu.VMEM((PASSES, total_planes + 1, tall, LANES), jnp.float32),
+            pltpu.VMEM((PASSES + 1, total_planes + 1, tall, LANES), jnp.float32),
+            pltpu.VMEM((PASSES + 1, total_planes + 1, tall, LANES), jnp.float32),
+            pltpu.VMEM((8, TILE, LANES), jnp.float32),
+            pltpu.VMEM((chunks + 1, 4, strip, LANES), jnp.float32),
+            pltpu.SemaphoreType.DMA,
+            pltpu.SemaphoreType.DMA,
+            pltpu.SemaphoreType.DMA((depth_count, chunks)),
+            pltpu.SemaphoreType.DMA((depth_count, chunks)),
+            pltpu.SemaphoreType.DMA((2,)),
+            pltpu.SemaphoreType.DMA((depth_count,)),
+        ],
+        compiler_params=pltpu.CompilerParams(
+            collective_id=0, has_side_effects=True, vmem_limit_bytes=56 * 2**20
+        ),
+    )(density, transfer_table)
+
+
+def fits_one_kernel(depth_count, rows_count, density):
+    planes, band, columns = density.shape
+    strip = band // depth_count
+    total_planes = planes * depth_count
+    return (
+        depth_count > 1
+        and rows_count > 1
+        and band % depth_count == 0
+        and strip % TILE == 0
+        and HALO * 2 == TILE
+        and columns % LANES == 0
+        and total_planes % UNROLL == 0
+        and planes * columns * band + 24 * (total_planes + 1) * (strip + TILE) * LANES < 2**22
+    )
+
+
+def choose(density, transfer_table):
+    depth_count = lax.axis_size("depth")
+    rows_count = lax.axis_size("rows")
+    if fits_one_kernel(depth_count, rows_count, density):
+        return in_one_kernel(depth_count, rows_count, density, transfer_table)
+    return per_device(density, transfer_table)
+
+
 def solution(mesh):
     placed = (P("depth", "rows", None), P())
     return jax.shard_map(
-        per_device,
+        choose,
         mesh=mesh,
         in_specs=placed,
         out_specs=P(None, ("rows", "depth"), None),

time: 180 us -> 38.2 us (0.21)
  waiting for transfers between devices: 66.7 us -> 0 us
  other arithmetic: 53.8 us -> 0 us
  starting transfers between devices: 51 us -> 0 us
  Pallas kernels: 0 us -> 36.5 us
  local copies, waits for them, and re-layouts: 6.58 us -> 1.57 us
    ppermute x19 -> x0, waiting for transfers between devices: 66.7 us -> none  [the longest x8 27.5 us: extended(): lax.ppermute(tail, axis, [(i, (i + 1) % count) for i in range(ends)])]
    ppermute x19 -> x0, starting transfers between devices: 51 us -> none  [the longest x8 33.7 us: extended(): lax.ppermute(tail, axis, [(i, (i + 1) % count) for i in range(ends)])]
    pallas_call x0 -> x1, Pallas kernels: none -> 36.5 us  [in_one_kernel(): pl.pallas_call(functools.partial(volume_kernel, depth_count, rows_count),...]
    another operation x4 -> x0, other arithmetic: 35.3 us -> none  [appearance(): jnp.stack([mixed[0] * shading, mixed[1] * shading, mixed[2] * shading])]
    sub x1 -> x0, other arithmetic: 12.8 us -> none  [appearance(): opacity = 1.0 - jnp.exp(-mixed[3] * (OPTICAL_DEPTH / depth_count))]
    slice x22 -> x0, local copies, waits for them, and re-layouts: 6.5 us -> none  [the longest x4 2.86 us: appearance(): transfer_table[channel, knot] * hat_weight]
    add x4 -> x0, other arithmetic: 3 us -> none  [the longest x2 2.58 us: diffusion_flux(): return center + TIME_STEP * summed]
  transfers between devices with their start and end apart: 19 -> 0, of which waited for: 15 -> 0; matrix products, arithmetic and copies ran while one was open for 3% -> 0% of each run, Pallas kernels for 0% -> 0%
where the time goes in v1:
time: 38.2 us; the launch traced here: 38.1 us
  Pallas kernels  36.5 us (96%)
  local copies, waits for them, and re-layouts  1.57 us (4%)
    pallas_call x1, Pallas kernels, in_one_kernel(): pl.pallas_call(functools.partial(volume_kernel, depth_count, rows_count),...  36.5 us
    unnamed x1, local copies, waits for them, and re-layouts  1.57 us

profile of v1, /device:TPU:0, one launch (start us, length us, event | category | flops | bytes accessed | tf_op | source)
XLA Modules:
  0.0 38.1 jit_solution(15096559116558579906)
XLA Ops:
  0.0 36.5 %shard_map.28 = f32[4,16,512]{2,1,0:T(8,128)} custom-call(f32[2,128,512]{2,1,0:T(8,128)} %density.1, f32[4,16]{1,0:T(4,128)} %transfer_table.1), custom_call_target="tpu_custom_call" | custom-call | tf_op jit(solution)/shard_map/pallas_call | solution.py:442
  36.5 1.6 %copy.4 = f32[4,16,512]{2,1,0:T(8,128)} copy(f32[4,16,512]{2,1,0:T(8,128)} %shard_map.28) | data formatting | bytes 262144

commit v2 on v1

--- a/solution.py
+++ b/solution.py
@@ -127,7 +127,7 @@
 HALO = PASSES + 1
 TILE = 8
 LANES = 128
-UNROLL = 4
+UNROLL = 16
 
 
 def flux(change):
@@ -338,10 +338,7 @@
             for u in range(UNROLL):
                 carry, result = plane(block * UNROLL + u, carry)
 
-            @pl.when(block == total_planes // UNROLL - 1)
-            def _():
-                later[p, total_planes] = result
-
+            later[p, total_planes] = result
             return carry
 
         here, center = cells(0)
@@ -442,7 +439,7 @@
     return pl.pallas_call(
         functools.partial(volume_kernel, depth_count, rows_count),
         out_shape=jax.ShapeDtypeStruct((4, strip, columns), jnp.float32),
-        in_specs=[pl.BlockSpec(memory_space=pl.ANY)] * 2,
+        in_specs=[pl.BlockSpec(memory_space=pltpu.HBM)] * 2,
         out_specs=pl.BlockSpec(memory_space=pltpu.VMEM),
         scratch_shapes=[
             pltpu.VMEM((planes, band, columns), jnp.float32),
@@ -463,7 +460,7 @@
             pltpu.SemaphoreType.DMA((depth_count,)),
         ],
         compiler_params=pltpu.CompilerParams(
-            collective_id=0, has_side_effects=True, vmem_limit_bytes=56 * 2**20
+            collective_id=0, has_side_effects=True, vmem_limit_bytes=24 * 2**20
         ),
     )(density, transfer_table)
 

time: 38.2 us -> 32.4 us (0.85)
  Pallas kernels: 36.5 us -> 29.8 us
  local copies, waits for them, and re-layouts: 1.57 us -> 2.38 us
    pallas_call x1, Pallas kernels: 36.5 us -> 29.8 us  [in_one_kernel(): pl.pallas_call(functools.partial(volume_kernel, depth_count, rows_count),...]
    unnamed x1 -> x5, local copies, waits for them, and re-layouts: 1.57 us -> 2.38 us
where the time goes in v2:
time: 32.4 us; the launch traced here: 32.2 us
  Pallas kernels  29.8 us (92%)
  local copies, waits for them, and re-layouts  2.38 us (7%)
    pallas_call x1, Pallas kernels, in_one_kernel(): pl.pallas_call(functools.partial(volume_kernel, depth_count, rows_count),...  29.8 us
    unnamed x5, local copies, waits for them, and re-layouts  2.38 us

profile of v2, /device:TPU:0, one launch (start us, length us, event | category | flops | bytes accessed | tf_op | source)
XLA Modules:
  0.0 32.2 jit_solution(8714555975941165881)
XLA Ops:
  0.0 0.0 copy-start
  0.0 1.0 %copy-done = f32[2,128,512]{2,1,0:T(8,128)S(1)} copy-done((f32[2,128,512]{2,1,0:T(8,128)S(1)}, f32[2,128,512]{2,1,0:T(8,128)}, u32[]{:S(2)}) %copy-start) | copy-done | bytes 524312
  1.0 0.0 copy-start.1
  1.0 0.7 %copy-done.1 = f32[4,16]{1,0:T(4,128)S(1)} copy-done((f32[4,16]{1,0:T(4,128)S(1)}, f32[4,16]{1,0:T(4,128)}, u32[]{:S(2)}) %copy-start.1) | copy-done | bytes 280
  1.7 29.8 %shard_map.28 = f32[4,16,512]{2,1,0:T(8,128)S(1)} custom-call(f32[2,128,512]{2,1,0:T(8,128)S(1)} %copy-done, f32[4,16]{1,0:T(4,128)S(1)} %copy-done.1), custom_call_target="tpu_custom_call" | custom-call | tf_op jit(solution)/shard_map/pallas_call | solution.py:439
  31.5 0.7 %copy.4 = f32[4,16,512]{2,1,0:T(8,128)} copy(f32[4,16,512]{2,1,0:T(8,128)S(1)} %shard_map.28) | data formatting | bytes 262144
Async XLA Ops:
  0.0 1.0 %copy-start = (f32[2,128,512]{2,1,0:T(8,128)S(1)}, f32[2,128,512]{2,1,0:T(8,128)}, u32[]{:S(2)}) copy-start(f32[2,128,512]{2,1,0:T(8,128)} %density.1) | copy-start | bytes 1572868
  1.0 0.7 %copy-start.1 = (f32[4,16]{1,0:T(4,128)S(1)}, f32[4,16]{1,0:T(4,128)}, u32[]{:S(2)}) copy-start(f32[4,16]{1,0:T(4,128)} %transfer_table.1) | copy-start | bytes 772

commit v3 on v2

--- a/solution.py
+++ b/solution.py
@@ -265,7 +265,6 @@
 
     @pl.loop(0, total_planes + 1)
     def _(z):
-        field[chunks, z] = dark
         for p in range(PASSES + 1):
             rolled[p, z] = dark
             side[p, z] = dark
@@ -300,9 +299,7 @@
             landing(edges.at[s], edge_recv.at[s]).wait()
 
     def stage(c, p):
-        low = jnp.where(c == 0, p, -1)
-        high = jnp.where(c == chunks, p, LANES)
-        inner = (lane > low) & (lane < high)
+        inner = lane > jnp.where(c == 0, p, -1)
 
         def cells(z):
             here = field[c, z] if p == 0 else later[p - 1, z]
@@ -344,6 +341,76 @@
         here, center = cells(0)
         lax.fori_loop(0, total_planes // UNROLL, step, (here, center, dark))
 
+    def transfer(cells):
+        position = cells * ((KNOTS - 1) / UPPER_DENSITY)
+        index = jnp.clip(position.astype(jnp.int32), 0, KNOTS - 2)
+        part = position - index.astype(jnp.float32)
+        tiles = [index[i : i + TILE] for i in range(0, strip, TILE)]
+        mixed = []
+        for channel in range(4):
+            value = jnp.concatenate([lookup(knots[channel], tile) for tile in tiles], axis=0)
+            slope = jnp.concatenate([lookup(knots[4 + channel], tile) for tile in tiles], axis=0)
+            mixed.append(value + part * slope)
+        return mixed
+
+    def shading_of(grad_depth, grad_row, grad_col):
+        return AMBIENT + (1.0 - AMBIENT) * jnp.abs(
+            0.64 * grad_depth + 0.6 * grad_row + 0.48 * grad_col
+        ) * lax.rsqrt(
+            grad_depth * grad_depth + grad_row * grad_row + grad_col * grad_col + 0.25
+        )
+
+    def last_columns():
+        group = LANES // total_planes
+        first_lane = lane < group
+        deepest = lane >= LANES - group
+        rightmost = lane % group == group - 1
+        cells = field[chunks - 1, total_planes - 1]
+        for z in range(total_planes - 1):
+            other = roll(field[chunks - 1, z], (z + 1) * group, 1)
+            cells = jnp.where((lane >= z * group) & (lane < (z + 1) * group), other, cells)
+
+        def changes(cells):
+            return (
+                roll(cells, -group, 1) - cells,
+                roll(cells, -1, 0) - cells,
+                roll(cells, -1, 1) - cells,
+            )
+
+        for sweep in range(PASSES):
+            below, down, right = changes(cells)
+            below = jnp.where(deepest, 0.0, flux(below))
+            down = flux(down)
+            right = jnp.where(rightmost, 0.0, flux(right))
+            summed = (
+                (below - roll(below, group, 1))
+                + (down - roll(down, 1, 0))
+                + (right - roll(right, 1, 1))
+            )
+            cells = cells + TIME_STEP * summed
+        below, down, right = changes(cells)
+        below = jnp.where(deepest, 0.0, below)
+        right = jnp.where(rightmost, 0.0, right)
+        shading = shading_of(
+            (below + roll(below, group, 1))[:strip] * 0.5,
+            (down + roll(down, 1, 0))[:strip] * 0.5,
+            (right + roll(right, 1, 1))[:strip] * 0.5,
+        )
+        mixed = transfer(cells[:strip])
+        through = jnp.exp(mixed[3] * (-OPTICAL_DEPTH / total_planes))
+        ahead = [group * 2**i for i in range((total_planes - 1).bit_length())]
+        for shift in ahead:
+            through = through * jnp.where(lane[:strip] < shift, 1.0, roll(through, shift, 1))
+        remaining = jnp.where(first_lane[:strip], 1.0, roll(through, group, 1))
+        weight = (remaining - through) * shading
+        result = []
+        for channel in range(3):
+            color = weight * mixed[channel]
+            for shift in ahead:
+                color = color + roll(color, shift, 1)
+            result.append(color)
+        return result + [through]
+
     def shade(c):
         cells, sides = stage(c, PASSES)
 
@@ -356,21 +423,8 @@
             grad_depth = (center_below[:strip] - nearer) * 0.5
             grad_row = (down + roll(down, 1, 0))[:strip] * 0.5
             grad_col = (right + left)[:strip] * 0.5
-            shading = AMBIENT + (1.0 - AMBIENT) * jnp.abs(
-                0.64 * grad_depth + 0.6 * grad_row + 0.48 * grad_col
-            ) * lax.rsqrt(
-                grad_depth * grad_depth + grad_row * grad_row + grad_col * grad_col + 0.25
-            )
-            position = middle * ((KNOTS - 1) / UPPER_DENSITY)
-            index = jnp.clip(position.astype(jnp.int32), 0, KNOTS - 2)
-            part = position - index.astype(jnp.float32)
-            tiles = [index[i : i + TILE] for i in range(0, strip, TILE)]
-            mixed = [
-                jnp.concatenate([lookup(knots[channel], tile) for tile in tiles], axis=0)
-                + part
-                * jnp.concatenate([lookup(knots[4 + channel], tile) for tile in tiles], axis=0)
-                for channel in range(4)
-            ]
+            shading = shading_of(grad_depth, grad_row, grad_col)
+            mixed = transfer(middle)
             through = jnp.exp(mixed[3] * (-OPTICAL_DEPTH / total_planes))
             kept = remaining * through
             weight = (remaining - kept) * shading
@@ -388,39 +442,34 @@
         carry = lax.fori_loop(0, total_planes // UNROLL, step, carry)
         for channel in range(3):
             shifted[c, channel] = carry[4][channel]
-        shifted[c, 3] = 1.0 - carry[3]
-
-    @pl.loop(0, chunks + 1)
+        shifted[c, 3] = carry[3]
+
+    @pl.loop(0, chunks)
     def _(c):
-        @pl.when(c < chunks)
+        for k in order:
+            source = lax.rem(d + k, depth_count)
+            landing(field.at[c, pl.ds(source * planes, planes)], recv.at[source, c]).wait()
+
+        @pl.when(d == 0)
         def _():
-            for k in order:
-                source = lax.rem(d + k, depth_count)
-                landing(
-                    field.at[c, pl.ds(source * planes, planes)], recv.at[source, c]
-                ).wait()
-
-            @pl.when(d == 0)
-            def _():
-                merge(c, jnp.logical_and(jnp.logical_not(upper), r > 0))
-
-            @pl.when(d == depth_count - 1)
-            def _():
-                merge(c, jnp.logical_and(upper, r < rows_count - 1))
-
-            field[c, total_planes] = field[c, total_planes - 1]
-
+            merge(c, jnp.logical_and(jnp.logical_not(upper), r > 0))
+
+        @pl.when(d == depth_count - 1)
+        def _():
+            merge(c, jnp.logical_and(upper, r < rows_count - 1))
+
+        field[c, total_planes] = field[c, total_planes - 1]
         for p in range(PASSES):
             diffuse(c, p)
         shade(c)
 
-    early = lax.broadcasted_iota(jnp.int32, (strip, LANES), 1) < LANES - HALO
+    ending = last_columns()
+    early = lane[:strip] < LANES - HALO
     for c in range(chunks):
         for channel in range(4):
+            beyond = roll(shifted[c + 1, channel], -HALO, 1) if c < chunks - 1 else ending[channel]
             picture[channel, :, c * LANES : (c + 1) * LANES] = jnp.where(
-                early,
-                roll(shifted[c, channel], -HALO, 1),
-                roll(shifted[c + 1, channel], -HALO, 1),
+                early, roll(shifted[c, channel], -HALO, 1), beyond
             )
 
     for c in range(chunks):
@@ -446,12 +495,12 @@
             pltpu.SMEM(transfer_table.shape, jnp.float32),
             pltpu.VMEM((depth_count, chunks, planes, tall, LANES), jnp.float32),
             pltpu.VMEM((depth_count + 1, planes, chunks, TILE, LANES), jnp.float32),
-            pltpu.VMEM((chunks + 1, total_planes + 1, tall, LANES), jnp.float32),
+            pltpu.VMEM((chunks, total_planes + 1, tall, LANES), jnp.float32),
             pltpu.VMEM((PASSES, total_planes + 1, tall, LANES), jnp.float32),
             pltpu.VMEM((PASSES + 1, total_planes + 1, tall, LANES), jnp.float32),
             pltpu.VMEM((PASSES + 1, total_planes + 1, tall, LANES), jnp.float32),
             pltpu.VMEM((8, TILE, LANES), jnp.float32),
-            pltpu.VMEM((chunks + 1, 4, strip, LANES), jnp.float32),
+            pltpu.VMEM((chunks, 4, strip, LANES), jnp.float32),
             pltpu.SemaphoreType.DMA,
             pltpu.SemaphoreType.DMA,
             pltpu.SemaphoreType.DMA((depth_count, chunks)),
@@ -460,7 +509,7 @@
             pltpu.SemaphoreType.DMA((depth_count,)),
         ],
         compiler_params=pltpu.CompilerParams(
-            collective_id=0, has_side_effects=True, vmem_limit_bytes=24 * 2**20
+            collective_id=0, has_side_effects=True, vmem_limit_bytes=56 * 2**20
         ),
     )(density, transfer_table)
 
@@ -477,6 +526,7 @@
         and HALO * 2 == TILE
         and columns % LANES == 0
         and total_planes % UNROLL == 0
+        and total_planes * 2 * HALO == LANES
         and planes * columns * band + 24 * (total_planes + 1) * (strip + TILE) * LANES < 2**22
     )
 
@@ -485,7 +535,9 @@
     depth_count = lax.axis_size("depth")
     rows_count = lax.axis_size("rows")
     if fits_one_kernel(depth_count, rows_count, density):
-        return in_one_kernel(depth_count, rows_count, density, transfer_table)
+        result = in_one_kernel(depth_count, rows_count, density, transfer_table)
+        last = lax.broadcasted_iota(jnp.int32, result.shape, 0) == 3
+        return jnp.where(last, 1.0 - result, result)
     return per_device(density, transfer_table)
 
 

time: 32.4 us -> 31.6 us (0.975)
  local copies, waits for them, and re-layouts: 2.38 us -> 0 us
  other arithmetic: 0 us -> 1.64 us
    unnamed x5 -> x0, local copies, waits for them, and re-layouts: 2.38 us -> none
    select_n x0 -> x1, other arithmetic: none -> 1.64 us  [choose(): return jnp.where(last, 1.0 - result, result)]
where the time goes in v3:
time: 31.6 us; the launch traced here: 31.5 us
  Pallas kernels  29.8 us (94%)
  other arithmetic  1.64 us (5%)
    pallas_call x1, Pallas kernels, in_one_kernel(): pl.pallas_call(functools.partial(volume_kernel, depth_count, rows_count),...  29.8 us
    select_n x1, other arithmetic, choose(): return jnp.where(last, 1.0 - result, result)  1.64 us

profile of v3, /device:TPU:0, one launch (start us, length us, event | category | flops | bytes accessed | tf_op | source)
XLA Modules:
  0.0 31.5 jit_solution(15956062285817598026)
XLA Ops:
  0.0 29.8 %shard_map.28 = f32[4,16,512]{2,1,0:T(8,128)} custom-call(f32[2,128,512]{2,1,0:T(8,128)} %density.1, f32[4,16]{1,0:T(4,128)} %transfer_table.1), custom_call_target="tpu_custom_call" | custom-call | tf_op jit(solution)/shard_map/pallas_call | solution.py:488
  29.8 1.6 %subtract_select_fusion = f32[4,16,512]{2,1,0:T(8,128)} fusion(f32[4,16,512]{2,1,0:T(8,128)} %shard_map.28, pred[4]{0:T(512)(128)(4,1)S(1)} %iota_compare_fusion), kind=kLoop, calls=%fused_computation | loop fusion | flops 65536 | bytes 262148 | tf_op jit(solution)/shard_map/jit(_where)/select_n | solution.py:540
  (1 shorter events, 0.0 us)

commit v4 on v3

--- a/solution.py
+++ b/solution.py
@@ -177,6 +177,10 @@
     next_rows = lax.rem(r + 1, rows_count)
     prev_rows = lax.rem(r + rows_count - 1, rows_count)
     order = sorted(range(1, depth_count), key=lambda k: abs(k - depth_count // 2))
+    odd = lax.rem(d, 2)
+
+    def peer_of(k):
+        return lax.rem(d + k + odd * (depth_count - 2 * k), depth_count)
 
     load = pltpu.make_async_copy(density, local, load_sem)
     load.start()
@@ -191,7 +195,7 @@
         )
 
     for k in order:
-        greet(lax.rem(d + k, depth_count), r)
+        greet(peer_of(k), r)
 
     @pl.when(d == 0)
     def _():
@@ -256,7 +260,7 @@
         copy.start()
     for c in range(chunks):
         for k in order:
-            parcel(lax.rem(d + k, depth_count), c, k).start()
+            parcel(peer_of(k), c, k).start()
 
     for c in range(chunks):
         for p in range(planes):
@@ -409,7 +413,7 @@
             for shift in ahead:
                 color = color + roll(color, shift, 1)
             result.append(color)
-        return result + [through]
+        return result + [1.0 - through]
 
     def shade(c):
         cells, sides = stage(c, PASSES)
@@ -442,7 +446,7 @@
         carry = lax.fori_loop(0, total_planes // UNROLL, step, carry)
         for channel in range(3):
             shifted[c, channel] = carry[4][channel]
-        shifted[c, 3] = carry[3]
+        shifted[c, 3] = 1.0 - carry[3]
 
     @pl.loop(0, chunks)
     def _(c):
@@ -474,7 +478,7 @@
 
     for c in range(chunks):
         for k in order:
-            parcel(lax.rem(d + k, depth_count), c, k).wait_send()
+            parcel(peer_of(k), c, k).wait_send()
     for copy in edge_copies():
         copy.wait_send()
 
@@ -509,9 +513,9 @@
             pltpu.SemaphoreType.DMA((depth_count,)),
         ],
         compiler_params=pltpu.CompilerParams(
-            collective_id=0, has_side_effects=True, vmem_limit_bytes=56 * 2**20
+            collective_id=0, has_side_effects=True, vmem_limit_bytes=24 * 2**20
         ),
-    )(density, transfer_table)
+    )(*[pltpu.with_memory_space_constraint(x, pltpu.HBM) for x in (density, transfer_table)])
 
 
 def fits_one_kernel(depth_count, rows_count, density):
@@ -535,9 +539,7 @@
     depth_count = lax.axis_size("depth")
     rows_count = lax.axis_size("rows")
     if fits_one_kernel(depth_count, rows_count, density):
-        result = in_one_kernel(depth_count, rows_count, density, transfer_table)
-        last = lax.broadcasted_iota(jnp.int32, result.shape, 0) == 3
-        return jnp.where(last, 1.0 - result, result)
+        return in_one_kernel(depth_count, rows_count, density, transfer_table)
     return per_device(density, transfer_table)
 
 

time: 31.6 us -> 30.2 us (0.956)
  other arithmetic: 1.64 us -> 0 us
  local copies, waits for them, and re-layouts: 0 us -> 0.66 us
  Pallas kernels: 29.8 us -> 29.4 us
    select_n x1 -> x0, other arithmetic: 1.64 us -> none  [choose(): return jnp.where(last, 1.0 - result, result)]
    unnamed x0 -> x1, local copies, waits for them, and re-layouts: none -> 0.66 us
    pallas_call x1, Pallas kernels: 29.8 us -> 29.4 us  [in_one_kernel(): pl.pallas_call(functools.partial(volume_kernel, depth_count, rows_count),...]
where the time goes in v4:
time: 30.2 us; the launch traced here: 30 us
  Pallas kernels  29.4 us (97%)
  local copies, waits for them, and re-layouts  0.66 us (2%)
    pallas_call x1, Pallas kernels, in_one_kernel(): pl.pallas_call(functools.partial(volume_kernel, depth_count, rows_count),...  29.4 us
    unnamed x1, local copies, waits for them, and re-layouts  0.66 us

profile of v4, /device:TPU:0, one launch (start us, length us, event | category | flops | bytes accessed | tf_op | source)
XLA Modules:
  0.0 30.0 jit_solution(17471254063543287503)
XLA Ops:
  0.0 29.4 %shard_map.28 = f32[4,16,512]{2,1,0:T(8,128)S(1)} custom-call(f32[2,128,512]{2,1,0:T(8,128)} %density.1, f32[4,16]{1,0:T(4,128)} %transfer_table.1), custom_call_target="tpu_custom_call" | custom-call | tf_op jit(solution)/shard_map/pallas_call | solution.py:492
  29.4 0.7 %copy.4 = f32[4,16,512]{2,1,0:T(8,128)} copy(f32[4,16,512]{2,1,0:T(8,128)S(1)} %shard_map.28) | data formatting | bytes 262144

commit v5 on v4

--- a/solution.py
+++ b/solution.py
@@ -160,6 +160,7 @@
     side,
     knots,
     shifted,
+    ending,
     load_sem,
     table_sem,
     send,
@@ -216,7 +217,9 @@
         for p in range(planes):
             first = local[p, :TILE, lanes]
             final = local[p, band - TILE :, lanes]
-            edges[depth_count, p, c] = jnp.concatenate([first[:HALO], final[HALO:]], axis=0)
+            at = p % 2 * HALO
+            edges[depth_count, p // 2, c, at : at + HALO, :] = first[:HALO]
+            edges[depth_count + 1, p // 2, c, at : at + HALO, :] = final[HALO:]
             for s in range(depth_count):
                 parcels[s, c, p, :strip, :] = local[p, s * strip : (s + 1) * strip, lanes]
                 if s == 0:
@@ -242,7 +245,7 @@
     def edge_copies():
         return [
             pltpu.make_async_remote_copy(
-                src_ref=edges.at[depth_count],
+                src_ref=edges.at[depth_count + slot],
                 dst_ref=edges.at[d],
                 send_sem=edge_send.at[slot],
                 recv_sem=edge_recv.at[d],
@@ -289,13 +292,13 @@
     lane_zero = lane == 0
     upper = lax.broadcasted_iota(jnp.int32, (TILE, LANES), 0) < HALO
 
-    def merge(c, replaced):
+    def merge(c, first_plane, replaced):
         for s in range(depth_count):
             for p in range(planes):
                 z = s * planes + p
-                field[c, z, strip:, :] = jnp.where(
-                    replaced, edges[s, p, c], field[c, z, strip:, :]
-                )
+                pair = edges[s, p // 2, c]
+                rows = pair if p % 2 == first_plane else roll(pair, HALO, 0)
+                field[c, z, strip:, :] = jnp.where(replaced, rows, field[c, z, strip:, :])
 
     @pl.when((d == 0) | (d == depth_count - 1))
     def _():
@@ -364,14 +367,14 @@
             grad_depth * grad_depth + grad_row * grad_row + grad_col * grad_col + 0.25
         )
 
-    def last_columns():
+    def last_columns(c):
         group = LANES // total_planes
         first_lane = lane < group
         deepest = lane >= LANES - group
         rightmost = lane % group == group - 1
-        cells = field[chunks - 1, total_planes - 1]
+        cells = field[c, total_planes - 1]
         for z in range(total_planes - 1):
-            other = roll(field[chunks - 1, z], (z + 1) * group, 1)
+            other = roll(field[c, z], (z + 1) * group, 1)
             cells = jnp.where((lane >= z * group) & (lane < (z + 1) * group), other, cells)
 
         def changes(cells):
@@ -407,13 +410,12 @@
             through = through * jnp.where(lane[:strip] < shift, 1.0, roll(through, shift, 1))
         remaining = jnp.where(first_lane[:strip], 1.0, roll(through, group, 1))
         weight = (remaining - through) * shading
-        result = []
         for channel in range(3):
             color = weight * mixed[channel]
             for shift in ahead:
                 color = color + roll(color, shift, 1)
-            result.append(color)
-        return result + [1.0 - through]
+            ending[channel] = color
+        ending[3] = 1.0 - through
 
     def shade(c):
         cells, sides = stage(c, PASSES)
@@ -456,18 +458,18 @@
 
         @pl.when(d == 0)
         def _():
-            merge(c, jnp.logical_and(jnp.logical_not(upper), r > 0))
+            merge(c, 1, jnp.logical_and(jnp.logical_not(upper), r > 0))
 
         @pl.when(d == depth_count - 1)
         def _():
-            merge(c, jnp.logical_and(upper, r < rows_count - 1))
+            merge(c, 0, jnp.logical_and(upper, r < rows_count - 1))
 
         field[c, total_planes] = field[c, total_planes - 1]
+        last_columns(c)
         for p in range(PASSES):
             diffuse(c, p)
         shade(c)
 
-    ending = last_columns()
     early = lane[:strip] < LANES - HALO
     for c in range(chunks):
         for channel in range(4):
@@ -498,13 +500,14 @@
             pltpu.VMEM((planes, band, columns), jnp.float32),
             pltpu.SMEM(transfer_table.shape, jnp.float32),
             pltpu.VMEM((depth_count, chunks, planes, tall, LANES), jnp.float32),
-            pltpu.VMEM((depth_count + 1, planes, chunks, TILE, LANES), jnp.float32),
+            pltpu.VMEM((depth_count + 2, planes // 2, chunks, TILE, LANES), jnp.float32),
             pltpu.VMEM((chunks, total_planes + 1, tall, LANES), jnp.float32),
             pltpu.VMEM((PASSES, total_planes + 1, tall, LANES), jnp.float32),
             pltpu.VMEM((PASSES + 1, total_planes + 1, tall, LANES), jnp.float32),
             pltpu.VMEM((PASSES + 1, total_planes + 1, tall, LANES), jnp.float32),
             pltpu.VMEM((8, TILE, LANES), jnp.float32),
             pltpu.VMEM((chunks, 4, strip, LANES), jnp.float32),
+            pltpu.VMEM((4, strip, LANES), jnp.float32),
             pltpu.SemaphoreType.DMA,
             pltpu.SemaphoreType.DMA,
             pltpu.SemaphoreType.DMA((depth_count, chunks)),
@@ -529,6 +532,7 @@
         and strip % TILE == 0
         and HALO * 2 == TILE
         and columns % LANES == 0
+        and planes % 2 == 0
         and total_planes % UNROLL == 0
         and total_planes * 2 * HALO == LANES
         and planes * columns * band + 24 * (total_planes + 1) * (strip + TILE) * LANES < 2**22

time: 30.2 us -> 30 us (level)
  no operation moved by 1% of the time
where the time goes in v5:
time: 30 us; the launch traced here: 29.9 us
  Pallas kernels  29.2 us (97%)
  local copies, waits for them, and re-layouts  0.66 us (2%)
    pallas_call x1, Pallas kernels, in_one_kernel(): pl.pallas_call(functools.partial(volume_kernel, depth_count, rows_count),...  29.2 us
    unnamed x1, local copies, waits for them, and re-layouts  0.66 us

profile of v5, /device:TPU:0, one launch (start us, length us, event | category | flops | bytes accessed | tf_op | source)
XLA Modules:
  0.0 29.9 jit_solution(16987407299313230447)
XLA Ops:
  0.0 29.2 %shard_map.28 = f32[4,16,512]{2,1,0:T(8,128)S(1)} custom-call(f32[2,128,512]{2,1,0:T(8,128)} %density.1, f32[4,16]{1,0:T(4,128)} %transfer_table.1), custom_call_target="tpu_custom_call" | custom-call | tf_op jit(solution)/shard_map/pallas_call | solution.py:494
  29.2 0.7 %copy.4 = f32[4,16,512]{2,1,0:T(8,128)} copy(f32[4,16,512]{2,1,0:T(8,128)S(1)} %shard_map.28) | data formatting | bytes 262144

commit v6 on v5

--- a/solution.py
+++ b/solution.py
@@ -183,8 +183,17 @@
     def peer_of(k):
         return lax.rem(d + k + odd * (depth_count - 2 * k), depth_count)
 
-    load = pltpu.make_async_copy(density, local, load_sem)
-    load.start()
+    def columns_of(c):
+        return slice(c * LANES, (c + 1) * LANES)
+
+    loads = [
+        pltpu.make_async_copy(
+            density.at[:, :, columns_of(c)], local.at[:, :, columns_of(c)], load_sem.at[c]
+        )
+        for c in range(chunks)
+    ]
+    for load in loads:
+        load.start()
     load_table = pltpu.make_async_copy(transfer_table, table, table_sem)
     load_table.start()
 
@@ -211,15 +220,24 @@
     def flipped(rows, first):
         return jnp.concatenate([rows[first - i : first - i + 1] for i in range(HALO)], axis=0)
 
-    load.wait()
-    for c in range(chunks):
-        lanes = slice(c * LANES, (c + 1) * LANES)
+    def parcel(peer, c, slot):
+        return pltpu.make_async_remote_copy(
+            src_ref=parcels.at[peer, c],
+            dst_ref=field.at[c, pl.ds(d * planes, planes)],
+            send_sem=send.at[slot, c],
+            recv_sem=recv.at[d, c],
+            device_id=(peer, r),
+            device_id_type=pl.DeviceIdType.MESH,
+        )
+
+    def build(c):
+        lanes = columns_of(c)
         for p in range(planes):
             first = local[p, :TILE, lanes]
             final = local[p, band - TILE :, lanes]
             at = p % 2 * HALO
-            edges[depth_count, p // 2, c, at : at + HALO, :] = first[:HALO]
-            edges[depth_count + 1, p // 2, c, at : at + HALO, :] = final[HALO:]
+            edges[depth_count, c, p // 2, at : at + HALO, :] = first[:HALO]
+            edges[depth_count + 1, c, p // 2, at : at + HALO, :] = final[HALO:]
             for s in range(depth_count):
                 parcels[s, c, p, :strip, :] = local[p, s * strip : (s + 1) * strip, lanes]
                 if s == 0:
@@ -232,23 +250,13 @@
                     after = local[p, (s + 1) * strip : (s + 1) * strip + TILE, lanes][:HALO]
                 parcels[s, c, p, strip:, :] = jnp.concatenate([after, before], axis=0)
 
-    def parcel(peer, c, slot):
-        return pltpu.make_async_remote_copy(
-            src_ref=parcels.at[peer, c],
-            dst_ref=field.at[c, pl.ds(d * planes, planes)],
-            send_sem=send.at[slot, c],
-            recv_sem=recv.at[d, c],
-            device_id=(peer, r),
-            device_id_type=pl.DeviceIdType.MESH,
-        )
-
-    def edge_copies():
+    def edge_copies(c):
         return [
             pltpu.make_async_remote_copy(
-                src_ref=edges.at[depth_count + slot],
-                dst_ref=edges.at[d],
-                send_sem=edge_send.at[slot],
-                recv_sem=edge_recv.at[d],
+                src_ref=edges.at[depth_count + slot, c],
+                dst_ref=edges.at[d, c],
+                send_sem=edge_send.at[slot, c],
+                recv_sem=edge_recv.at[d, c],
                 device_id=(depth, rows),
                 device_id_type=pl.DeviceIdType.MESH,
             )
@@ -258,12 +266,15 @@
     def landing(ref, sem):
         return pltpu.make_async_copy(ref, ref, sem)
 
-    pl.semaphore_wait(barrier, depth_count + 1)
-    for copy in edge_copies():
-        copy.start()
     for c in range(chunks):
+        loads[c].wait()
+        build(c)
+        if c == 0:
+            pl.semaphore_wait(barrier, depth_count + 1)
         for k in order:
             parcel(peer_of(k), c, k).start()
+        for copy in edge_copies(c):
+            copy.start()
 
     for c in range(chunks):
         for p in range(planes):
@@ -294,16 +305,12 @@
 
     def merge(c, first_plane, replaced):
         for s in range(depth_count):
+            landing(edges.at[s, c], edge_recv.at[s, c]).wait()
             for p in range(planes):
                 z = s * planes + p
-                pair = edges[s, p // 2, c]
+                pair = edges[s, c, p // 2]
                 rows = pair if p % 2 == first_plane else roll(pair, HALO, 0)
                 field[c, z, strip:, :] = jnp.where(replaced, rows, field[c, z, strip:, :])
-
-    @pl.when((d == 0) | (d == depth_count - 1))
-    def _():
-        for s in range(depth_count):
-            landing(edges.at[s], edge_recv.at[s]).wait()
 
     def stage(c, p):
         inner = lane > jnp.where(c == 0, p, -1)
@@ -481,8 +488,8 @@
     for c in range(chunks):
         for k in order:
             parcel(peer_of(k), c, k).wait_send()
-    for copy in edge_copies():
-        copy.wait_send()
+        for copy in edge_copies(c):
+            copy.wait_send()
 
 
 def in_one_kernel(depth_count, rows_count, density, transfer_table):
@@ -500,7 +507,7 @@
             pltpu.VMEM((planes, band, columns), jnp.float32),
             pltpu.SMEM(transfer_table.shape, jnp.float32),
             pltpu.VMEM((depth_count, chunks, planes, tall, LANES), jnp.float32),
-            pltpu.VMEM((depth_count + 2, planes // 2, chunks, TILE, LANES), jnp.float32),
+            pltpu.VMEM((depth_count + 2, chunks, planes // 2, TILE, LANES), jnp.float32),
             pltpu.VMEM((chunks, total_planes + 1, tall, LANES), jnp.float32),
             pltpu.VMEM((PASSES, total_planes + 1, tall, LANES), jnp.float32),
             pltpu.VMEM((PASSES + 1, total_planes + 1, tall, LANES), jnp.float32),
@@ -508,12 +515,12 @@
             pltpu.VMEM((8, TILE, LANES), jnp.float32),
             pltpu.VMEM((chunks, 4, strip, LANES), jnp.float32),
             pltpu.VMEM((4, strip, LANES), jnp.float32),
-            pltpu.SemaphoreType.DMA,
+            pltpu.SemaphoreType.DMA((chunks,)),
             pltpu.SemaphoreType.DMA,
             pltpu.SemaphoreType.DMA((depth_count, chunks)),
             pltpu.SemaphoreType.DMA((depth_count, chunks)),
-            pltpu.SemaphoreType.DMA((2,)),
-            pltpu.SemaphoreType.DMA((depth_count,)),
+            pltpu.SemaphoreType.DMA((2, chunks)),
+            pltpu.SemaphoreType.DMA((depth_count, chunks)),
         ],
         compiler_params=pltpu.CompilerParams(
             collective_id=0, has_side_effects=True, vmem_limit_bytes=24 * 2**20

time: 30 us -> 31.5 us (1.050)
  Pallas kernels: 29.2 us -> 30.7 us
    pallas_call x1, Pallas kernels: 29.2 us -> 30.7 us  [in_one_kernel(): pl.pallas_call(functools.partial(volume_kernel, depth_count, rows_count),...]
where the time goes in v6:
time: 31.5 us; the launch traced here: 31.4 us
  Pallas kernels  30.7 us (97%)
  local copies, waits for them, and re-layouts  0.66 us (2%)
    pallas_call x1, Pallas kernels, in_one_kernel(): pl.pallas_call(functools.partial(volume_kernel, depth_count, rows_count),...  30.7 us
    unnamed x1, local copies, waits for them, and re-layouts  0.66 us

profile of v6, /device:TPU:0, one launch (start us, length us, event | category | flops | bytes accessed | tf_op | source)
XLA Modules:
  0.0 31.4 jit_solution(3743648552602479579)
XLA Ops:
  0.0 30.7 %shard_map.28 = f32[4,16,512]{2,1,0:T(8,128)S(1)} custom-call(f32[2,128,512]{2,1,0:T(8,128)} %density.1, f32[4,16]{1,0:T(4,128)} %transfer_table.1), custom_call_target="tpu_custom_call" | custom-call | tf_op jit(solution)/shard_map/pallas_call | solution.py:501
  30.7 0.7 %copy.4 = f32[4,16,512]{2,1,0:T(8,128)} copy(f32[4,16,512]{2,1,0:T(8,128)S(1)} %shard_map.28) | data formatting | bytes 262144

commit v7 on v5

--- a/solution.py
+++ b/solution.py
@@ -128,6 +128,7 @@
 TILE = 8
 LANES = 128
 UNROLL = 16
+GROUP = 2
 
 
 def flux(change):
@@ -232,12 +233,12 @@
                     after = local[p, (s + 1) * strip : (s + 1) * strip + TILE, lanes][:HALO]
                 parcels[s, c, p, strip:, :] = jnp.concatenate([after, before], axis=0)
 
-    def parcel(peer, c, slot):
+    def parcel(peer, g, slot):
         return pltpu.make_async_remote_copy(
-            src_ref=parcels.at[peer, c],
-            dst_ref=field.at[c, pl.ds(d * planes, planes)],
-            send_sem=send.at[slot, c],
-            recv_sem=recv.at[d, c],
+            src_ref=parcels.at[peer, pl.ds(g * GROUP, GROUP)],
+            dst_ref=field.at[pl.ds(g * GROUP, GROUP), pl.ds(d * planes, planes)],
+            send_sem=send.at[slot, g],
+            recv_sem=recv.at[d, g],
             device_id=(peer, r),
             device_id_type=pl.DeviceIdType.MESH,
         )
@@ -261,9 +262,9 @@
     pl.semaphore_wait(barrier, depth_count + 1)
     for copy in edge_copies():
         copy.start()
-    for c in range(chunks):
+    for g in range(chunks // GROUP):
         for k in order:
-            parcel(peer_of(k), c, k).start()
+            parcel(peer_of(k), g, k).start()
 
     for c in range(chunks):
         for p in range(planes):
@@ -452,9 +453,14 @@
 
     @pl.loop(0, chunks)
     def _(c):
-        for k in order:
-            source = lax.rem(d + k, depth_count)
-            landing(field.at[c, pl.ds(source * planes, planes)], recv.at[source, c]).wait()
+        @pl.when(lax.rem(c, GROUP) == 0)
+        def _():
+            for k in order:
+                source = lax.rem(d + k, depth_count)
+                landing(
+                    field.at[pl.ds(c, GROUP), pl.ds(source * planes, planes)],
+                    recv.at[source, lax.div(c, GROUP)],
+                ).wait()
 
         @pl.when(d == 0)
         def _():
@@ -478,9 +484,9 @@
                 early, roll(shifted[c, channel], -HALO, 1), beyond
             )
 
-    for c in range(chunks):
+    for g in range(chunks // GROUP):
         for k in order:
-            parcel(peer_of(k), c, k).wait_send()
+            parcel(peer_of(k), g, k).wait_send()
     for copy in edge_copies():
         copy.wait_send()
 
@@ -510,8 +516,8 @@
             pltpu.VMEM((4, strip, LANES), jnp.float32),
             pltpu.SemaphoreType.DMA,
             pltpu.SemaphoreType.DMA,
-            pltpu.SemaphoreType.DMA((depth_count, chunks)),
-            pltpu.SemaphoreType.DMA((depth_count, chunks)),
+            pltpu.SemaphoreType.DMA((depth_count, chunks // GROUP)),
+            pltpu.SemaphoreType.DMA((depth_count, chunks // GROUP)),
             pltpu.SemaphoreType.DMA((2,)),
             pltpu.SemaphoreType.DMA((depth_count,)),
         ],
@@ -531,7 +537,7 @@
         and band % depth_count == 0
         and strip % TILE == 0
         and HALO * 2 == TILE
-        and columns % LANES == 0
+        and columns % (GROUP * LANES) == 0
         and planes % 2 == 0
         and total_planes % UNROLL == 0
         and total_planes * 2 * HALO == LANES

time: 30 us -> 31.2 us (1.040)
  Pallas kernels: 29.2 us -> 30.4 us
    pallas_call x1, Pallas kernels: 29.2 us -> 30.4 us  [in_one_kernel(): pl.pallas_call(functools.partial(volume_kernel, depth_count, rows_count),...]
where the time goes in v7:
time: 31.2 us; the launch traced here: 31.1 us
  Pallas kernels  30.4 us (97%)
  local copies, waits for them, and re-layouts  0.66 us (2%)
    pallas_call x1, Pallas kernels, in_one_kernel(): pl.pallas_call(functools.partial(volume_kernel, depth_count, rows_count),...  30.4 us
    unnamed x1, local copies, waits for them, and re-layouts  0.66 us

profile of v7, /device:TPU:0, one launch (start us, length us, event | category | flops | bytes accessed | tf_op | source)
XLA Modules:
  0.0 31.1 jit_solution(15527955735382334909)
XLA Ops:
  0.0 30.4 %shard_map.28 = f32[4,16,512]{2,1,0:T(8,128)S(1)} custom-call(f32[2,128,512]{2,1,0:T(8,128)} %density.1, f32[4,16]{1,0:T(4,128)} %transfer_table.1), custom_call_target="tpu_custom_call" | custom-call | tf_op jit(solution)/shard_map/pallas_call | solution.py:500
  30.4 0.7 %copy.4 = f32[4,16,512]{2,1,0:T(8,128)} copy(f32[4,16,512]{2,1,0:T(8,128)S(1)} %shard_map.28) | data formatting | bytes 262144

commit v8 on v5

--- a/solution.py
+++ b/solution.py
@@ -450,8 +450,23 @@
             shifted[c, channel] = carry[4][channel]
         shifted[c, 3] = 1.0 - carry[3]
 
+    early = lane[:strip] < LANES - HALO
+
+    def write(c, channel, beyond):
+        lanes = pl.ds(pl.multiple_of(c * LANES, LANES), LANES) if not isinstance(c, int) else slice(c * LANES, (c + 1) * LANES)
+        own = roll(shifted[c, channel], -HALO, 1)
+        picture[channel, :, lanes] = jnp.where(early, own, beyond)
+
+    def finish_sends(c):
+        for k in order:
+            parcel(peer_of(k), c, k).wait_send()
+
     @pl.loop(0, chunks)
     def _(c):
+        @pl.when(c > 0)
+        def _():
+            finish_sends(c - 1)
+
         for k in order:
             source = lax.rem(d + k, depth_count)
             landing(field.at[c, pl.ds(source * planes, planes)], recv.at[source, c]).wait()
@@ -470,17 +485,14 @@
             diffuse(c, p)
         shade(c)
 
-    early = lane[:strip] < LANES - HALO
-    for c in range(chunks):
-        for channel in range(4):
-            beyond = roll(shifted[c + 1, channel], -HALO, 1) if c < chunks - 1 else ending[channel]
-            picture[channel, :, c * LANES : (c + 1) * LANES] = jnp.where(
-                early, roll(shifted[c, channel], -HALO, 1), beyond
-            )
-
-    for c in range(chunks):
-        for k in order:
-            parcel(peer_of(k), c, k).wait_send()
+        @pl.when(c > 0)
+        def _():
+            for channel in range(4):
+                write(c - 1, channel, roll(shifted[c, channel], -HALO, 1))
+
+    for channel in range(4):
+        write(chunks - 1, channel, ending[channel])
+    finish_sends(chunks - 1)
     for copy in edge_copies():
         copy.wait_send()
 

time: 30 us -> 30.2 us (level)
  no operation moved by 1% of the time
where the time goes in v8:
time: 30.2 us; the launch traced here: 30 us
  Pallas kernels  29.4 us (97%)
  local copies, waits for them, and re-layouts  0.66 us (2%)
    pallas_call x1, Pallas kernels, in_one_kernel(): pl.pallas_call(functools.partial(volume_kernel, depth_count, rows_count),...  29.4 us
    unnamed x1, local copies, waits for them, and re-layouts  0.66 us

profile of v8, /device:TPU:0, one launch (start us, length us, event | category | flops | bytes accessed | tf_op | source)
XLA Modules:
  0.0 30.0 jit_solution(1962121361978988626)
XLA Ops:
  0.0 29.4 %shard_map.28 = f32[4,16,512]{2,1,0:T(8,128)S(1)} custom-call(f32[2,128,512]{2,1,0:T(8,128)} %density.1, f32[4,16]{1,0:T(4,128)} %transfer_table.1), custom_call_target="tpu_custom_call" | custom-call | tf_op jit(solution)/shard_map/pallas_call | solution.py:506
  29.4 0.7 %copy.4 = f32[4,16,512]{2,1,0:T(8,128)} copy(f32[4,16,512]{2,1,0:T(8,128)S(1)} %shard_map.28) | data formatting | bytes 262144

commit v9 on v8

--- a/solution.py
+++ b/solution.py
@@ -151,6 +151,7 @@
     transfer_table,
     picture,
     local,
+    rim,
     table,
     parcels,
     edges,
@@ -183,8 +184,20 @@
     def peer_of(k):
         return lax.rem(d + k + odd * (depth_count - 2 * k), depth_count)
 
-    load = pltpu.make_async_copy(density, local, load_sem)
-    load.start()
+    rims = [
+        pltpu.make_async_copy(density.at[:, :TILE, :], rim.at[0], load_sem.at[chunks]),
+        pltpu.make_async_copy(density.at[:, band - TILE :, :], rim.at[1], load_sem.at[chunks + 1]),
+    ]
+    loads = [
+        pltpu.make_async_copy(
+            density.at[:, :, c * LANES : (c + 1) * LANES],
+            local.at[:, :, c * LANES : (c + 1) * LANES],
+            load_sem.at[c],
+        )
+        for c in range(chunks)
+    ]
+    for load in rims + loads:
+        load.start()
     load_table = pltpu.make_async_copy(transfer_table, table, table_sem)
     load_table.start()
 
@@ -211,15 +224,21 @@
     def flipped(rows, first):
         return jnp.concatenate([rows[first - i : first - i + 1] for i in range(HALO)], axis=0)
 
-    load.wait()
-    for c in range(chunks):
+    def parcel(peer, c, slot):
+        return pltpu.make_async_remote_copy(
+            src_ref=parcels.at[peer, c],
+            dst_ref=field.at[c, pl.ds(d * planes, planes)],
+            send_sem=send.at[slot, c],
+            recv_sem=recv.at[d, c],
+            device_id=(peer, r),
+            device_id_type=pl.DeviceIdType.MESH,
+        )
+
+    def build(c):
         lanes = slice(c * LANES, (c + 1) * LANES)
         for p in range(planes):
             first = local[p, :TILE, lanes]
             final = local[p, band - TILE :, lanes]
-            at = p % 2 * HALO
-            edges[depth_count, p // 2, c, at : at + HALO, :] = first[:HALO]
-            edges[depth_count + 1, p // 2, c, at : at + HALO, :] = final[HALO:]
             for s in range(depth_count):
                 parcels[s, c, p, :strip, :] = local[p, s * strip : (s + 1) * strip, lanes]
                 if s == 0:
@@ -231,16 +250,6 @@
                 else:
                     after = local[p, (s + 1) * strip : (s + 1) * strip + TILE, lanes][:HALO]
                 parcels[s, c, p, strip:, :] = jnp.concatenate([after, before], axis=0)
-
-    def parcel(peer, c, slot):
-        return pltpu.make_async_remote_copy(
-            src_ref=parcels.at[peer, c],
-            dst_ref=field.at[c, pl.ds(d * planes, planes)],
-            send_sem=send.at[slot, c],
-            recv_sem=recv.at[d, c],
-            device_id=(peer, r),
-            device_id_type=pl.DeviceIdType.MESH,
-        )
 
     def edge_copies():
         return [
@@ -258,10 +267,21 @@
     def landing(ref, sem):
         return pltpu.make_async_copy(ref, ref, sem)
 
-    pl.semaphore_wait(barrier, depth_count + 1)
-    for copy in edge_copies():
-        copy.start()
+    for load in rims:
+        load.wait()
+    for p in range(planes):
+        at = p % 2 * HALO
+        for c in range(chunks):
+            lanes = slice(c * LANES, (c + 1) * LANES)
+            edges[depth_count, p // 2, c, at : at + HALO, :] = rim[0, p, :, lanes][:HALO]
+            edges[depth_count + 1, p // 2, c, at : at + HALO, :] = rim[1, p, :, lanes][HALO:]
     for c in range(chunks):
+        loads[c].wait()
+        build(c)
+        if c == 0:
+            pl.semaphore_wait(barrier, depth_count + 1)
+            for copy in edge_copies():
+                copy.start()
         for k in order:
             parcel(peer_of(k), c, k).start()
 
@@ -510,6 +530,7 @@
         out_specs=pl.BlockSpec(memory_space=pltpu.VMEM),
         scratch_shapes=[
             pltpu.VMEM((planes, band, columns), jnp.float32),
+            pltpu.VMEM((2, planes, TILE, columns), jnp.float32),
             pltpu.SMEM(transfer_table.shape, jnp.float32),
             pltpu.VMEM((depth_count, chunks, planes, tall, LANES), jnp.float32),
             pltpu.VMEM((depth_count + 2, planes // 2, chunks, TILE, LANES), jnp.float32),
@@ -520,7 +541,7 @@
             pltpu.VMEM((8, TILE, LANES), jnp.float32),
             pltpu.VMEM((chunks, 4, strip, LANES), jnp.float32),
             pltpu.VMEM((4, strip, LANES), jnp.float32),
-            pltpu.SemaphoreType.DMA,
+            pltpu.SemaphoreType.DMA((chunks + 2,)),
             pltpu.SemaphoreType.DMA,
             pltpu.SemaphoreType.DMA((depth_count, chunks)),
             pltpu.SemaphoreType.DMA((depth_count, chunks)),

time: 30.2 us -> 30.2 us (level)
  no operation moved by 1% of the time
where the time goes in v9:
time: 30.2 us; the launch traced here: 30.1 us
  Pallas kernels  29.4 us (97%)
  local copies, waits for them, and re-layouts  0.66 us (2%)
    pallas_call x1, Pallas kernels, in_one_kernel(): pl.pallas_call(functools.partial(volume_kernel, depth_count, rows_count),...  29.4 us
    unnamed x1, local copies, waits for them, and re-layouts  0.66 us

profile of v9, /device:TPU:0, one launch (start us, length us, event | category | flops | bytes accessed | tf_op | source)
XLA Modules:
  0.0 30.1 jit_solution(6880673444788605336)
XLA Ops:
  0.0 29.4 %shard_map.28 = f32[4,16,512]{2,1,0:T(8,128)S(1)} custom-call(f32[2,128,512]{2,1,0:T(8,128)} %density.1, f32[4,16]{1,0:T(4,128)} %transfer_table.1), custom_call_target="tpu_custom_call" | custom-call | tf_op jit(solution)/shard_map/pallas_call | solution.py:526
  29.4 0.7 %copy.4 = f32[4,16,512]{2,1,0:T(8,128)} copy(f32[4,16,512]{2,1,0:T(8,128)S(1)} %shard_map.28) | data formatting | bytes 262144

commit v10 on v8

--- a/solution.py
+++ b/solution.py
@@ -177,7 +177,8 @@
     r = lax.axis_index("rows")
     next_rows = lax.rem(r + 1, rows_count)
     prev_rows = lax.rem(r + rows_count - 1, rows_count)
-    order = sorted(range(1, depth_count), key=lambda k: abs(k - depth_count // 2))
+    far = sorted(range(1, depth_count), key=lambda k: abs(k - depth_count // 2))
+    order = [far[i // 2] if i % 2 == 0 else far[-1 - i // 2] for i in range(depth_count - 1)]
     odd = lax.rem(d, 2)
 
     def peer_of(k):

time: 30.2 us -> 30.8 us (1.020)
  Pallas kernels: 29.4 us -> 30 us
    pallas_call x1, Pallas kernels: 29.4 us -> 30 us  [in_one_kernel(): pl.pallas_call(functools.partial(volume_kernel, depth_count, rows_count),...]
where the time goes in v10:
time: 30.8 us; the launch traced here: 30.7 us
  Pallas kernels  30 us (97%)
  local copies, waits for them, and re-layouts  0.66 us (2%)
    pallas_call x1, Pallas kernels, in_one_kernel(): pl.pallas_call(functools.partial(volume_kernel, depth_count, rows_count),...  30 us
    unnamed x1, local copies, waits for them, and re-layouts  0.66 us

profile of v10, /device:TPU:0, one launch (start us, length us, event | category | flops | bytes accessed | tf_op | source)
XLA Modules:
  0.0 30.7 jit_solution(8965521992931229514)
XLA Ops:
  0.0 30.0 %shard_map.28 = f32[4,16,512]{2,1,0:T(8,128)S(1)} custom-call(f32[2,128,512]{2,1,0:T(8,128)} %density.1, f32[4,16]{1,0:T(4,128)} %transfer_table.1), custom_call_target="tpu_custom_call" | custom-call | tf_op jit(solution)/shard_map/pallas_call | solution.py:507
  30.0 0.7 %copy.4 = f32[4,16,512]{2,1,0:T(8,128)} copy(f32[4,16,512]{2,1,0:T(8,128)S(1)} %shard_map.28) | data formatting | bytes 262144
